TPU v7x, 512 devices: a whole 4x4x16 slice. The times are simulated.
512 devices in a mesh: gx: 16 (over x, z_hi, core), gy: 32 (over y, z_lo).
Axes of the slice: x: 4, y: 4, z: 16 (z_hi: 2, z_lo: 8; z = z_hi * 8 + z_lo), core: 2. Of those that a mesh axis runs over, the one named last changes fastest.
Arguments:
- positions: float32 [3, 64, 1024, 128], P(None, 'gx', 'gy'), may hold values from 0 to 1
- velocities: float32 [3, 64, 1024, 128], P(None, 'gx', 'gy'), may hold values from -4 to 4
- counts: int32 [64, 1024], P('gx', 'gy'), may hold values from 40 to 128, as said below
- cell_pairs: int32 [16, 32, 640], P('gx', 'gy'), may hold values from 0 to 639, as said below
- pair_count: int32 [16, 32], P('gx', 'gy'), may hold values from 128 to 640, as said below
Outputs:
- density: float32 [64, 1024, 128], P('gx', 'gy')
- accel: float32 [3, 64, 1024, 128], P(None, 'gx', 'gy')
Inputs may be any that keep to these rules, and one draw needn't show every extreme that they name: `counts`: each device's block of cells holds at least one cell with 128 particles. `cell_pairs`: entry c names cell c // 5 of the device's 4 x 32 block in row-major order and partner kind c % 5. The first pair_count entries of a device are distinct, include the pair of each of its cells with itself, and their partners lie inside the 64 x 1024 grid; the other entries are 0. `pair_count`: some device lists all 640 of its pairs.
All inputs are finite; a program needn't handle non-finite values.
Results may differ from a plain program's by a relative error of at most 0.0003.
Values sent between devices are 32-bit elements; how exact they have to be, the bound alone decides.
A program may use at most 64 MiB of HBM per device.

v0:
```python
import jax
import jax.numpy as jnp
from jax import lax
from jax.sharding import PartitionSpec as P

SMOOTH = 0.5
NORMAL = 21.0 / (16.0 * 3.141592653589793 * SMOOTH**3)
PARTICLE_MASS = 1.0 / 128.0
REST_DENSITY = 0.5
SOUND_SPEED = 0.5
VISCOUS = 0.3
GRAVITY = 1.0
block_pairs = 16


def with_halo(array, sides, width):
    for axis, dim in sides:
        size, length = (lax.axis_size(axis), array.shape[dim])
        up = [(i, (i + 1) % size) for i in range(size - 1)]
        down = [(j, i) for i, j in up]
        last = lax.slice_in_dim(array, length - width, length, axis=dim)
        first = lax.slice_in_dim(array, 0, width, axis=dim)
        before = lax.ppermute(last, axis, up)
        after = lax.ppermute(first, axis, down)
        array = jnp.concatenate([before, array, after], axis=dim)
    return array


def passed_along(value, axis, steps):
    count = lax.axis_size(axis)
    first, last = (max(0, -steps), min(count, count - steps))
    return lax.ppermute(value, axis, [(source, source + steps) for source in range(first, last)])


def offsets(offset_kind):
    step_x = ((offset_kind == 1) | (offset_kind == 3) | (offset_kind == 4)).astype(jnp.int32)
    step_y = ((offset_kind == 2) | (offset_kind == 3)).astype(jnp.int32) - (
        offset_kind == 4
    ).astype(jnp.int32)
    return (step_x, step_y)


def separation(pos_a, pos_b, step_x, step_y):
    sep_x = pos_a[0][:, :, None] - pos_b[0][:, None, :] - step_x[:, None, None]
    sep_y = pos_a[1][:, :, None] - pos_b[1][:, None, :] - step_y[:, None, None]
    sep_z = pos_a[2][:, :, None] - pos_b[2][:, None, :]
    return (sep_x, sep_y, sep_z)


def pair_weights(occ_a, occ_b, live_flag, itself):
    diagonal = jnp.eye(occ_a.shape[1], dtype=jnp.float32)
    return (
        occ_a[:, :, None]
        * occ_b[:, None, :]
        * live_flag[:, None, None]
        * (1.0 - diagonal[None] * itself[:, None, None])
    )


def density_terms(pos_a, pos_b, occ_a, occ_b, step_x, step_y, live_flag, itself):
    sep_x, sep_y, sep_z = separation(pos_a, pos_b, step_x, step_y)
    distance = jnp.sqrt(sep_x * sep_x + sep_y * sep_y + sep_z * sep_z)
    support = jnp.maximum(1.0 - 0.5 * distance / SMOOTH, 0.0)
    weight = PARTICLE_MASS * NORMAL * support**4 * (1.0 + 2.0 * distance / SMOOTH)
    weight = weight * pair_weights(occ_a, occ_b, live_flag, itself)
    to_a = jnp.sum(weight, axis=2)
    to_b = jnp.sum(weight, axis=1) * (1.0 - itself)[:, None]
    return (to_a, to_b)


def force_terms(
    pos_a,
    pos_b,
    vel_a,
    vel_b,
    term_a,
    term_b,
    rho_a,
    rho_b,
    occ_a,
    occ_b,
    step_x,
    step_y,
    live_flag,
    itself,
):
    sep_x, sep_y, sep_z = separation(pos_a, pos_b, step_x, step_y)
    dist_sq = sep_x * sep_x + sep_y * sep_y + sep_z * sep_z
    distance = jnp.sqrt(dist_sq)
    support = jnp.maximum(1.0 - 0.5 * distance / SMOOTH, 0.0)
    gradient = -5.0 * NORMAL * support**3 / (SMOOTH * SMOOTH)
    closing = (vel_a[0][:, :, None] - vel_b[0][:, None, :]) * sep_x
    closing = closing + (vel_a[1][:, :, None] - vel_b[1][:, None, :]) * sep_y
    closing = closing + (vel_a[2][:, :, None] - vel_b[2][:, None, :]) * sep_z
    approach = SMOOTH * jnp.minimum(closing, 0.0) / (dist_sq + 0.01 * SMOOTH * SMOOTH)
    damping = -VISCOUS * SOUND_SPEED * approach / (0.5 * (rho_a[:, :, None] + rho_b[:, None, :]))
    scalar = PARTICLE_MASS * (term_a[:, :, None] + term_b[:, None, :] + damping) * gradient
    scalar = scalar * pair_weights(occ_a, occ_b, live_flag, itself)
    to_a = -jnp.stack(
        [
            jnp.sum(scalar * sep_x, axis=2),
            jnp.sum(scalar * sep_y, axis=2),
            jnp.sum(scalar * sep_z, axis=2),
        ]
    )
    keep_b = (1.0 - itself)[None, :, None]
    to_b = (
        jnp.stack(
            [
                jnp.sum(scalar * sep_x, axis=1),
                jnp.sum(scalar * sep_y, axis=1),
                jnp.sum(scalar * sep_z, axis=1),
            ]
        )
        * keep_b
    )
    return (to_a, to_b)


def extend(block_data):
    row_ext = with_halo(block_data, (("gy", 2),), 1)
    received = passed_along(row_ext[:, 0:1], "gx", -1)
    result = jnp.concatenate([row_ext, received], axis=1)
    return result


def give_back(partial_value):
    cells_x = partial_value.shape[1] - 1
    cells_y = partial_value.shape[2] - 2
    column = passed_along(partial_value[:, cells_x : cells_x + 1], "gx", 1)
    summed = partial_value.at[:, 0:1].add(column)
    edge_rows = jnp.concatenate(
        [summed[:, :cells_x, 0:1], summed[:, :cells_x, cells_y + 1 : cells_y + 2]], axis=2
    )
    arrived = with_halo(edge_rows, (("gy", 2),), 1)
    middle = summed[:, :cells_x, 1 : cells_y + 1]
    middle = middle.at[:, :, 0:1].add(arrived[:, :, 0:1])
    result = middle.at[:, :, cells_y - 1 : cells_y].add(arrived[:, :, 3:4])
    return result


def prepare_pairs(cell_pairs, pair_count, cells_y):
    pair_codes = cell_pairs.reshape(-1)
    live_total = pair_count.reshape(())
    width = pair_codes.shape[0]
    padded = (width + block_pairs - 1) // block_pairs * block_pairs
    cell_index = pair_codes // 5
    offset_kind = pair_codes % 5
    step_x, step_y = offsets(offset_kind)
    ext_span = cells_y + 2
    source = cell_index // cells_y * ext_span + cell_index % cells_y + 1
    target = (cell_index // cells_y + step_x) * ext_span + cell_index % cells_y + step_y + 1
    live_flag = (jnp.arange(padded, dtype=jnp.int32) < live_total).astype(jnp.float32)
    itself = (offset_kind == 0).astype(jnp.float32)
    rounds = (live_total + block_pairs - 1) // block_pairs
    return (
        source,
        target,
        step_x.astype(jnp.float32),
        step_y.astype(jnp.float32),
        live_flag,
        itself,
        rounds,
    )


def per_device(positions, velocities, counts, cell_pairs, pair_count):
    cells_x = positions.shape[1]
    cells_y = positions.shape[2]
    per_cell = positions.shape[3]
    ext_cells = (cells_x + 1) * (cells_y + 2)
    occupied = (jnp.arange(per_cell, dtype=jnp.int32)[None, None, :] < counts[:, :, None]).astype(
        jnp.float32
    )[None]
    outgoing = jnp.concatenate([positions, occupied], axis=0)
    extended = extend(outgoing).reshape(outgoing.shape[0], ext_cells, per_cell)
    pos_ext = extended[0:3]
    occ_ext = extended[3]
    source, target, step_x, step_y, live_flag, itself, rounds = prepare_pairs(
        cell_pairs, pair_count, cells_y
    )

    def select_rows(array, round_index):
        return lax.dynamic_slice_in_dim(array, round_index * block_pairs, block_pairs)

    def density_round(round_index, totals):
        src_rows = select_rows(source, round_index)
        dst_rows = select_rows(target, round_index)
        to_a, to_b = density_terms(
            pos_ext[:, src_rows],
            pos_ext[:, dst_rows],
            occ_ext[src_rows],
            occ_ext[dst_rows],
            select_rows(step_x, round_index),
            select_rows(step_y, round_index),
            select_rows(live_flag, round_index),
            select_rows(itself, round_index),
        )
        return totals.at[src_rows].add(to_a).at[dst_rows].add(to_b)

    totals = lax.fori_loop(0, rounds, density_round, jnp.zeros((ext_cells, per_cell), jnp.float32))
    returned = give_back(totals.reshape(1, cells_x + 1, cells_y + 2, per_cell))
    density = (PARTICLE_MASS * NORMAL + returned[0]) * occupied[0]
    second_ext = extend(jnp.concatenate([velocities, density[None]], axis=0)).reshape(
        4, ext_cells, per_cell
    )
    vel_ext = second_ext[0:3]
    rho_ext = second_ext[3]
    safe_rho = jnp.where(occ_ext > 0.0, rho_ext, 1.0)
    pressure_term = SOUND_SPEED * SOUND_SPEED * (safe_rho - REST_DENSITY) / (safe_rho * safe_rho)

    def force_round(round_index, forces):
        src_rows = select_rows(source, round_index)
        dst_rows = select_rows(target, round_index)
        to_a, to_b = force_terms(
            pos_ext[:, src_rows],
            pos_ext[:, dst_rows],
            vel_ext[:, src_rows],
            vel_ext[:, dst_rows],
            pressure_term[src_rows],
            pressure_term[dst_rows],
            safe_rho[src_rows],
            safe_rho[dst_rows],
            occ_ext[src_rows],
            occ_ext[dst_rows],
            select_rows(step_x, round_index),
            select_rows(step_y, round_index),
            select_rows(live_flag, round_index),
            select_rows(itself, round_index),
        )
        return forces.at[:, src_rows].add(to_a).at[:, dst_rows].add(to_b)

    forces = lax.fori_loop(0, rounds, force_round, jnp.zeros((3, ext_cells, per_cell), jnp.float32))
    own_forces = give_back(forces.reshape(3, cells_x + 1, cells_y + 2, per_cell))
    pull = jnp.array([0.0, 0.0, -GRAVITY], dtype=jnp.float32)[:, None, None, None]
    accel = (own_forces + pull) * occupied
    return (density, accel)


def solution(mesh):
    placed = (
        P(None, "gx", "gy", None),
        P(None, "gx", "gy", None),
        P("gx", "gy"),
        P("gx", "gy", None),
        P("gx", "gy"),
    )
    return jax.shard_map(
        per_device,
        mesh=mesh,
        in_specs=placed,
        out_specs=(P("gx", "gy", None), P(None, "gx", "gy", None)),
        check_vma=False,
    )
```

profile of v0, /device:TPU:30, one launch (start us, length us, event | category | flops | bytes accessed | tf_op | source)
XLA Modules:
  0.0 896.0 jit_solution(2005562538822466743)
XLA Ops:
  2.3 13.3 %collective-permute-start.1 = (f32[4,4,1,128]{3,2,1,0:T(1,128)S(1)}, f32[4,4,1,128]{3,2,1,0:T(1,128)S(1)}, u32[]{:S(2)}, u32[]{:S(2)}) collective-permute-start(f32[4,4,1,128]{3,2,1,0:T(1,128)S(1)} %get-tuple-element.493), channel_id=1, source_target_pairs={{1,0},{2,1},{3,2},{4,3},{5,4},{6,5},{7,6},{8,7},{9,8},{10,9},{11,1... | collective-permute-start | bytes 24584 | tf_op jit(solution)/shard_map/ppermute | solution.py:24
  18.3 10.4 %collective-permute-done = f32[4,4,1,128]{3,2,1,0:T(1,128)S(1)} collective-permute-done((f32[4,4,1,128]{3,2,1,0:T(1,128)S(1)}, f32[4,4,1,128]{3,2,1,0:T(1,128)S(1)}, u32[]{:S(2)}, u32[]{:S(2)}) %collective-permute-start) | collective-permute-done | bytes 8224 | tf_op jit(solution)/shard_map/ppermute | solution.py:23
  28.7 6.5 collective-permute-start.2
  37.5 244.2 %while.30 = (s32[]{:T(128)}, f32[170,128]{1,0:T(8,128)S(1)}, s32[]{:T(128)}, s32[640]{0:T(1024)S(1)}, f32[3,170,128]{2,0,1:T(4,128)S(1)}, /*index=5*/s32[640]{0:...) while((s32[]{:T(128)}, f32[170,128]{1,0:T(8,128)S(1)}, ...), condition=%wide.region_5.6_spmd, body=%wide.region_0.5_spmd.sunk | while | flops 6852726 | bytes 572631 | solution.py:201
  283.8 19.1 %collective-permute-done.3 = f32[1,1,34,128]{3,2,1,0:T(8,128)S(1)} collective-permute-done((f32[1,1,34,128]{3,2,1,0:T(8,128)S(1)}, f32[1,1,34,128]{3,2,1,0:T(8,128)S(1)}, u32[]{:S(2)}, u32[]{:S(2)}) %collective-permute-start.3) | collective-permute-done | bytes 17440 | tf_op jit(solution)/shard_map/ppermute | solution.py:32
  304.9 11.4 %collective-permute-start.5 = (f32[1,4,1,128]{3,2,1,0:T(1,128)S(1)}, f32[1,4,1,128]{3,2,1,0:T(1,128)S(1)}, u32[]{:S(2)}, u32[]{:S(2)}) collective-permute-start(f32[1,4,1,128]{3,2,1,0:T(1,128)S(1)} %get-tuple-element.494), channel_id=1, source_target_pairs={{1,0},{2,1},{3,2},{4,3},{5,4},{6,5},{7,6},{8,7},{9,8},{10,9},{11,1... | collective-permute-start | bytes 6152 | tf_op jit(solution)/shard_map/ppermute | solution.py:24
  318.4 11.7 %collective-permute-start.7 = (f32[4,4,1,128]{3,2,1,0:T(1,128)S(1)}, f32[4,4,1,128]{3,2,1,0:T(1,128)S(1)}, u32[]{:S(2)}, u32[]{:S(2)}) collective-permute-start(f32[4,4,1,128]{3,2,1,0:T(1,128)S(1)} %get-tuple-element.491), channel_id=1, source_target_pairs={{1,0},{2,1},{3,2},{4,3},{5,4},{6,5},{7,6},{8,7},{9,8},{10,9},{11,1... | collective-permute-start | bytes 24584 | tf_op jit(solution)/shard_map/ppermute | solution.py:24
  332.0 11.1 %collective-permute-done.6 = f32[4,4,1,128]{3,2,1,0:T(1,128)S(1)} collective-permute-done((f32[4,4,1,128]{3,2,1,0:T(1,128)S(1)}, f32[4,4,1,128]{3,2,1,0:T(1,128)S(1)}, u32[]{:S(2)}, u32[]{:S(2)}) %collective-permute-start.6) | collective-permute-done | bytes 8224 | tf_op jit(solution)/shard_map/ppermute | solution.py:23
  347.4 503.5 %while.31 = (s32[]{:T(128)}, f32[3,170,128]{2,0,1:T(4,128)S(1)}, s32[]{:T(128)}, s32[640]{0:T(1024)S(1)}, f32[170,128]{1,0:T(8,128)S(1)}, /*index=5*/s32[640]{0:...) while((s32[]{:T(128)}, f32[3,170,128]{2,0,1:T(4,128)S(1)}, ...), condition=%wide.region_15.16_spmd, body=%wide.region_6.15_spmd.sunk | while | flops 13178998 | bytes 1173743 | solution.py:233
  353.7 4.3 fusion.72
  366.6 4.3 fusion.72
  379.5 4.3 fusion.72
  392.4 4.3 fusion.72
  405.3 4.3 fusion.72
  418.2 4.3 fusion.72
  431.1 4.3 fusion.72
  444.0 4.3 fusion.72
  456.9 4.3 fusion.72
  469.9 4.3 fusion.72
  482.8 4.3 fusion.72
  495.7 4.3 fusion.72
  508.6 4.3 fusion.72
  521.5 4.3 fusion.72
  547.3 4.3 fusion.72
  560.2 4.3 fusion.72
  573.1 4.3 fusion.72
  586.1 4.3 fusion.72
  599.0 4.3 fusion.72
  611.9 4.3 fusion.72
  624.8 4.3 fusion.72
  637.7 4.3 fusion.72
  650.6 4.3 fusion.72
  663.5 4.3 fusion.72
  676.4 4.3 fusion.72
  689.3 4.3 fusion.72
  702.2 4.3 fusion.72
  715.1 4.3 fusion.72
  728.1 4.3 fusion.72
  753.9 4.3 fusion.72
  766.8 4.3 fusion.72
  779.7 4.3 fusion.72
  792.6 4.3 fusion.72
  805.5 4.3 fusion.72
  818.4 4.3 fusion.72
  831.3 4.3 fusion.72
  844.2 4.3 fusion.72
  853.0 26.1 %collective-permute-done.9 = f32[3,1,34,128]{3,2,1,0:T(8,128)S(1)} collective-permute-done((f32[3,1,34,128]{3,2,1,0:T(8,128)S(1)}, f32[3,1,34,128]{3,2,1,0:T(8,128)S(1)}, u32[]{:S(2)}, u32[]{:S(2)}) %collective-permute-start.9) | collective-permute-done | bytes 52256 | tf_op jit(solution)/shard_map/ppermute | solution.py:32
  881.8 11.4 %collective-permute-start.11 = (f32[3,4,1,128]{3,2,1,0:T(1,128)S(1)}, f32[3,4,1,128]{3,2,1,0:T(1,128)S(1)}, u32[]{:S(2)}, u32[]{:S(2)}) collective-permute-start(f32[3,4,1,128]{3,2,1,0:T(1,128)S(1)} %get-tuple-element.488), channel_id=1, source_target_pairs={{1,0},{2,1},{3,2},{4,3},{5,4},{6,5},{7,6},{8,7},{9,8},{10,9},{11,1... | collective-permute-start | bytes 18440 | tf_op jit(solution)/shard_map/ppermute | solution.py:24
  (1826 shorter events, 606.8 us)
Async XLA Ops:
  0.6 28.1 %copy-start = (f32[3,4,32,128]{3,2,1,0:T(8,128)S(1)}, f32[3,4,32,128]{3,2,1,0:T(8,128)}, u32[]{:S(2)}) copy-start(f32[3,4,32,128]{3,2,1,0:T(8,128)} %param.22) | copy-start | bytes 589828
  2.3 15.3 %copy-start.3 = (s32[1,1,640]{2,1,0:T(1,128)S(1)}, s32[1,1,640]{2,1,0:T(1,128)}, u32[]{:S(2)}) copy-start(s32[1,1,640]{2,1,0:T(1,128)} %param.25) | copy-start | bytes 7684
  2.3 16.0 %collective-permute-start.1 = (f32[4,4,1,128]{3,2,1,0:T(1,128)S(1)}, f32[4,4,1,128]{3,2,1,0:T(1,128)S(1)}, u32[]{:S(2)}, u32[]{:S(2)}) collective-permute-start(f32[4,4,1,128]{3,2,1,0:T(1,128)S(1)} %get-tuple-element.493), channel_id=1, source_target_pairs={{1,0},{2,1},{3,2},{4,3},{5,4},{6,5},{7,6},{8,7},{9,8},{10,9},{11,1... | collective-permute-start | bytes 24584 | tf_op jit(solution)/shard_map/ppermute | solution.py:24
  15.7 13.0 %collective-permute-start = (f32[4,4,1,128]{3,2,1,0:T(1,128)S(1)}, f32[4,4,1,128]{3,2,1,0:T(1,128)S(1)}, u32[]{:S(2)}, u32[]{:S(2)}) collective-permute-start(f32[4,4,1,128]{3,2,1,0:T(1,128)S(1)} %get-tuple-element.492), channel_id=1, source_target_pairs={{0,1},{1,2},{2,3},{3,4},{4,5},{5,6},{6,7},{7,8},{8,9},{9,10},{10,1... | collective-permute-start | bytes 24584 | tf_op jit(solution)/shard_map/ppermute | solution.py:23
  28.7 8.5 collective-permute-start.2
  281.7 36.6 %copy-start.1 = (f32[3,4,32,128]{3,2,1,0:T(8,128)S(1)}, f32[3,4,32,128]{3,2,1,0:T(8,128)}, u32[]{:S(2)}) copy-start(f32[3,4,32,128]{3,2,1,0:T(8,128)} %param.23) | copy-start | bytes 589828
  281.8 21.1 %collective-permute-start.3 = (f32[1,1,34,128]{3,2,1,0:T(8,128)S(1)}, f32[1,1,34,128]{3,2,1,0:T(8,128)S(1)}, u32[]{:S(2)}, u32[]{:S(2)}) collective-permute-start(f32[1,1,34,128]{3,2,1,0:T(8,128)S(1)} %slice.420), channel_id=1, source_target_pairs={{0,32},{32,64},{64,96},{96,128},{128,160},{160,192},{192,224},{224... | collective-permute-start | bytes 52232 | tf_op jit(solution)/shard_map/ppermute | solution.py:32
  302.9 13.4 %collective-permute-start.4 = (f32[1,4,1,128]{3,2,1,0:T(1,128)S(1)}, f32[1,4,1,128]{3,2,1,0:T(1,128)S(1)}, u32[]{:S(2)}, u32[]{:S(2)}) collective-permute-start(f32[1,4,1,128]{3,2,1,0:T(1,128)S(1)} %get-tuple-element.495), channel_id=1, source_target_pairs={{0,1},{1,2},{2,3},{3,4},{4,5},{5,6},{6,7},{7,8},{8,9},{9,10},{10,1... | collective-permute-start | bytes 6152 | tf_op jit(solution)/shard_map/ppermute | solution.py:23
  304.9 12.7 %collective-permute-start.5 = (f32[1,4,1,128]{3,2,1,0:T(1,128)S(1)}, f32[1,4,1,128]{3,2,1,0:T(1,128)S(1)}, u32[]{:S(2)}, u32[]{:S(2)}) collective-permute-start(f32[1,4,1,128]{3,2,1,0:T(1,128)S(1)} %get-tuple-element.494), channel_id=1, source_target_pairs={{1,0},{2,1},{3,2},{4,3},{5,4},{6,5},{7,6},{8,7},{9,8},{10,9},{11,1... | collective-permute-start | bytes 6152 | tf_op jit(solution)/shard_map/ppermute | solution.py:24
  317.6 0.7 copy-start.2
  318.4 13.6 %collective-permute-start.7 = (f32[4,4,1,128]{3,2,1,0:T(1,128)S(1)}, f32[4,4,1,128]{3,2,1,0:T(1,128)S(1)}, u32[]{:S(2)}, u32[]{:S(2)}) collective-permute-start(f32[4,4,1,128]{3,2,1,0:T(1,128)S(1)} %get-tuple-element.491), channel_id=1, source_target_pairs={{1,0},{2,1},{3,2},{4,3},{5,4},{6,5},{7,6},{8,7},{9,8},{10,9},{11,1... | collective-permute-start | bytes 24584 | tf_op jit(solution)/shard_map/ppermute | solution.py:24
  330.1 13.0 %collective-permute-start.6 = (f32[4,4,1,128]{3,2,1,0:T(1,128)S(1)}, f32[4,4,1,128]{3,2,1,0:T(1,128)S(1)}, u32[]{:S(2)}, u32[]{:S(2)}) collective-permute-start(f32[4,4,1,128]{3,2,1,0:T(1,128)S(1)} %get-tuple-element.490), channel_id=1, source_target_pairs={{0,1},{1,2},{2,3},{3,4},{4,5},{5,6},{6,7},{7,8},{8,9},{9,10},{10,1... | collective-permute-start | bytes 24584 | tf_op jit(solution)/shard_map/ppermute | solution.py:23
  343.2 4.0 collective-permute-start.8
  851.0 28.1 %collective-permute-start.9 = (f32[3,1,34,128]{3,2,1,0:T(8,128)S(1)}, f32[3,1,34,128]{3,2,1,0:T(8,128)S(1)}, u32[]{:S(2)}, u32[]{:S(2)}) collective-permute-start(f32[3,1,34,128]{3,2,1,0:T(8,128)S(1)} %slice.427), channel_id=1, source_target_pairs={{0,32},{32,64},{64,96},{96,128},{128,160},{160,192},{192,224},{224... | collective-permute-start | bytes 156680 | tf_op jit(solution)/shard_map/ppermute | solution.py:32
  879.1 14.1 %collective-permute-start.10 = (f32[3,4,1,128]{3,2,1,0:T(1,128)S(1)}, f32[3,4,1,128]{3,2,1,0:T(1,128)S(1)}, u32[]{:S(2)}, u32[]{:S(2)}) collective-permute-start(f32[3,4,1,128]{3,2,1,0:T(1,128)S(1)} %get-tuple-element.489), channel_id=1, source_target_pairs={{0,1},{1,2},{2,3},{3,4},{4,5},{5,6},{6,7},{7,8},{8,9},{9,10},{10,1... | collective-permute-start | bytes 18440 | tf_op jit(solution)/shard_map/ppermute | solution.py:23
  881.8 12.8 %collective-permute-start.11 = (f32[3,4,1,128]{3,2,1,0:T(1,128)S(1)}, f32[3,4,1,128]{3,2,1,0:T(1,128)S(1)}, u32[]{:S(2)}, u32[]{:S(2)}) collective-permute-start(f32[3,4,1,128]{3,2,1,0:T(1,128)S(1)} %get-tuple-element.488), channel_id=1, source_target_pairs={{1,0},{2,1},{3,2},{4,3},{5,4},{6,5},{7,6},{8,7},{9,8},{10,9},{11,1... | collective-permute-start | bytes 18440 | tf_op jit(solution)/shard_map/ppermute | solution.py:24
  894.5 0.7 copy-start.4
where the time goes:
time: 896 us
  other arithmetic  408 us (46%)
  local copies, waits for them, and re-layouts  338 us (38%)
  waiting for transfers between devices  73.1 us (8%)
  starting transfers between devices  67.9 us (8%)
    reduce_sum x39, other arithmetic, force_terms(): jnp.sum(scalar * sep_x, axis=1)  168 us
    scatter-add x78, other arithmetic, force_round(): return forces.at[:, src_rows].add(to_a).at[:, dst_rows].add(to_b)  85.2 us
    reduce_sum x39, other arithmetic, density_terms(): to_b = jnp.sum(weight, axis=1) * (1.0 - itself)[:, None]  77.1 us
    scatter-add x78, other arithmetic, density_round(): return totals.at[src_rows].add(to_a).at[dst_rows].add(to_b)  57.3 us
    ppermute x4, waiting for transfers between devices, passed_along(): lax.ppermute(value, axis, [(source, source + steps) for source in range(f...  49.2 us
    ppermute x4, starting transfers between devices, with_halo(): after = lax.ppermute(first, axis, down)  47.9 us
    gather x39, local copies, waits for them, and re-layouts, force_round(): vel_ext[:, dst_rows]  22.9 us
    gather x39, local copies, waits for them, and re-layouts, force_round(): pos_ext[:, dst_rows]  22.9 us
  transfers between devices with their start and end apart: 12, of which 8 were waited for; matrix products, arithmetic and copies ran while one was open for 0% of the time, Pallas kernels for 0%

commit v1 on v0

v1 whole, which is shorter than its diff:
```python
import functools

import jax
import jax.numpy as jnp
from jax import lax
from jax.experimental import pallas as pl
from jax.experimental.pallas import tpu as pltpu
from jax.sharding import PartitionSpec as P

SMOOTH = 0.5
NORMAL = 21.0 / (16.0 * 3.141592653589793 * SMOOTH**3)
PARTICLE_MASS = 1.0 / 128.0
REST_DENSITY = 0.5
SOUND_SPEED = 0.5
VISCOUS = 0.3
GRAVITY = 1.0
STEPS = ((0, 0), (1, 0), (0, 1), (1, 1), (1, -1))
FAR = 1.0e4
TINY = 1.0e-12
GROUP = 16
CLASSES = tuple(range(1, 9))


def rounded(value):
    return value.astype(jnp.bfloat16).astype(jnp.float32)


def pieces(value):
    high = rounded(value)
    rest = value - high
    middle = rounded(rest)
    return high, middle, rest - middle


def row_ids():
    return lax.broadcasted_iota(jnp.int32, (8, 128), 0)


def partner_block(block, step, far):
    ids = row_ids()
    step_x, step_y = step
    size = block[3:4] + far
    flow = block[7:8]
    moved = block
    if step_x:
        size = size + 2.0 * step_x * block[0:1]
        flow = flow + float(step_x) * block[4:5]
        moved = jnp.where(ids == 0, moved + float(step_x), moved)
    if step_y:
        size = size + 2.0 * step_y * block[1:2]
        flow = flow + float(step_y) * block[5:6]
        moved = jnp.where(ids == 1, moved + float(step_y), moved)
    size = size + float(step_x * step_x + step_y * step_y)
    moved = jnp.where(ids == 3, size, moved)
    if step_x or step_y:
        moved = jnp.where(ids == 7, flow, moved)
    return moved


def right_side(block):
    high, middle, low = pieces(block)
    ones = jnp.ones((8, 128), jnp.float32)
    zeros = jnp.zeros((8, 128), jnp.float32)
    return jnp.concatenate([high, middle, low, ones, high, middle, high, zeros], axis=0)


def left_blocks(form, own, extra):
    high, middle, low = pieces(form)
    ids = row_ids()
    own_high, own_middle, own_low = pieces(own)
    constant = jnp.where(ids == 0, own_high, jnp.where(ids == 1, own_middle, jnp.where(ids == 2, own_low, 0.0)))
    return [high, high, high, constant, middle, middle, low, extra]


def size_form(block):
    ids = row_ids()
    form = jnp.where(ids < 3, -2.0 * block, jnp.where(ids == 3, 1.0, 0.0))
    return form, block[3:4]


def flow_form(block):
    ids = row_ids()
    swapped = pltpu.roll(block, 4, 0)
    form = jnp.where(ids == 7, -1.0, jnp.where(ids == 3, 0.0, swapped))
    return form, -block[7:8]


def split(value):
    high = value.astype(jnp.bfloat16)
    return high, (value - high.astype(jnp.float32)).astype(jnp.bfloat16)


def dot(a, b):
    return jnp.dot(a, b, preferred_element_type=jnp.float32)


def dot_nt(a, b):
    return lax.dot_general(a, b, (((1,), (1,)), ((), ())), preferred_element_type=jnp.float32)


def by_class(count, body):
    needed = (count + GROUP - 1) // GROUP
    for group in CLASSES:
        pl.when(needed == group)(functools.partial(body, group * GROUP))


def density_kernel(cells, count_ref, far_ref, p_ref, out_ref, acc):
    cells_x, cells_y = cells
    span = cells_y + 2
    acc[...] = jnp.zeros_like(acc)
    ids = row_ids()
    first_row = jnp.where(ids == 0, 1.0, 0.0).astype(jnp.bfloat16)

    @pl.loop(0, cells_x * cells_y)
    def _(cell):
        home = cell // cells_y * span + cell % cells_y + 1
        block = p_ref[home]
        form, own = size_form(block)
        zeros = jnp.zeros((8, 128), jnp.float32)
        left = jnp.concatenate(left_blocks(form, own, zeros), axis=0).T.astype(jnp.bfloat16)
        homes = [home + step_x * span + step_y for step_x, step_y in STEPS]
        rights = []
        for kind, step in enumerate(STEPS):
            partner = partner_block(p_ref[homes[kind]], step, far_ref[cell * 5 + kind])
            rights.append(right_side(partner).astype(jnp.bfloat16))

        def body(rows):
            total = None
            for kind in range(5):
                square = dot(left[:rows], rights[kind])
                safe = jnp.maximum(square, TINY)
                near = jnp.maximum(1.0 - safe * lax.rsqrt(safe), 0.0)
                two = near * near
                weight = two * two * (5.0 - 4.0 * near)
                total = weight if total is None else total + weight
                if kind:
                    acc[homes[kind]] += jnp.sum(weight.reshape(rows // 8, 8, 128), axis=0)
            high, low = split(total)
            acc[home, :, :rows] += dot_nt(first_row, high) + dot_nt(first_row, low)

        by_class(count_ref[cell], body)

    out_ref[...] = (PARTICLE_MASS * NORMAL) * jnp.sum(acc[...], axis=1)


def force_kernel(cells, count_ref, far_ref, p_ref, rho_ref, term_ref, out_ref, acc):
    cells_x, cells_y = cells
    span = cells_y + 2
    acc[...] = jnp.zeros_like(acc)
    ids = row_ids()

    def place(block, row, col):
        base = jnp.where(ids == 0, row.astype(jnp.float32), 0.0) + jnp.where(ids == 1, col.astype(jnp.float32), 0.0)
        return jnp.where(ids < 3, block + base, jnp.where(ids == 3, 1.0, 0.0))

    def stacked(value):
        high, middle, low = pieces(value)
        zeros = jnp.zeros((8, 128), jnp.float32)
        return jnp.concatenate([high, middle, low, zeros], axis=0).astype(jnp.bfloat16)

    def joined(value):
        return value[0:8] + value[8:16] + value[16:24]

    @pl.loop(0, cells_x * cells_y)
    def _(cell):
        row = cell // cells_y
        col = cell % cells_y
        home = row * span + col + 1
        block = p_ref[home]
        rho_own = rho_ref[pl.ds(home, 1)]
        term_own = term_ref[pl.ds(home, 1)]
        zeros = jnp.zeros((8, 128), jnp.float32)
        extra = jnp.where(ids == 0, rho_own, jnp.where(ids == 1, term_own, 0.0))
        blocks = left_blocks(*size_form(block), extra) + left_blocks(*flow_form(block), zeros)
        turned = jnp.concatenate(blocks, axis=0).T
        left = turned.astype(jnp.bfloat16)
        rho_rows = turned[:, 56:57]
        term_rows = turned[:, 57:58]
        own_place = stacked(place(block, row, col))
        homes = [home + step_x * span + step_y for step_x, step_y in STEPS]
        rights = []
        places = []
        empty = jnp.zeros((64, 128), jnp.bfloat16)
        for kind, (step_x, step_y) in enumerate(STEPS):
            other = p_ref[homes[kind]]
            side = right_side(partner_block(other, (step_x, step_y), far_ref[cell * 5 + kind])).astype(jnp.bfloat16)
            rights.append(jnp.concatenate([jnp.concatenate([side, empty], axis=1), jnp.concatenate([empty, side], axis=1)], axis=0))
            places.append(stacked(place(other, row + step_x, col + step_y)))

        def body(rows):
            total = jnp.zeros((32, rows), jnp.float32)
            rho_i = jnp.broadcast_to(rho_rows[:rows], (rows, 128))
            term_i = jnp.broadcast_to(term_rows[:rows], (rows, 128))
            for kind in range(5):
                forms = dot(left[:rows], rights[kind])
                safe = jnp.maximum(forms[:, :128], TINY)
                near = jnp.maximum(1.0 - safe * lax.rsqrt(safe), 0.0)
                cubed = near * near * near
                rho_j = rho_ref[pl.ds(homes[kind], 1)]
                term_j = term_ref[pl.ds(homes[kind], 1)]
                bottom = (safe + 0.01 * SMOOTH * SMOOTH) * (rho_i + rho_j)
                damping = jnp.maximum(forms[:, 128:], 0.0) * pl.reciprocal(bottom, approx=True)
                scalar = (term_i + term_j + damping) * cubed
                high, low = split(scalar)
                total = total + dot_nt(places[kind], high) + dot_nt(places[kind], low)
                if kind:
                    column = dot(own_place[:, :rows], high) + dot(own_place[:, :rows], low)
                    acc[homes[kind]] += joined(column)
            acc[home, :, :rows] += joined(total)

        by_class(count_ref[cell], body)

    scale = PARTICLE_MASS * 5.0 * NORMAL / (SMOOTH * SMOOTH)

    @pl.loop(0, (cells_x + 1) * span)
    def _(cell):
        sums = acc[cell]
        here = place(p_ref[cell], cell // span, cell % span - 1)
        out_ref[cell] = scale * (here * sums[3:4] - sums)


def call_density(cells, count, far, extended):
    total = extended.shape[0]
    return pl.pallas_call(
        functools.partial(density_kernel, cells),
        out_shape=jax.ShapeDtypeStruct((total, 128), jnp.float32),
        in_specs=[
            pl.BlockSpec(memory_space=pltpu.SMEM),
            pl.BlockSpec(memory_space=pltpu.SMEM),
            pl.BlockSpec(memory_space=pltpu.VMEM),
        ],
        out_specs=pl.BlockSpec(memory_space=pltpu.VMEM),
        scratch_shapes=[pltpu.VMEM((total, 8, 128), jnp.float32)],
        compiler_params=pltpu.CompilerParams(vmem_limit_bytes=32 * 1024 * 1024),
        name="density",
    )(count, far, extended)


def call_force(cells, count, far, extended, rho, term):
    total = extended.shape[0]
    return pl.pallas_call(
        functools.partial(force_kernel, cells),
        out_shape=jax.ShapeDtypeStruct((total, 8, 128), jnp.float32),
        in_specs=[pl.BlockSpec(memory_space=pltpu.SMEM)] * 2 + [pl.BlockSpec(memory_space=pltpu.VMEM)] * 3,
        out_specs=pl.BlockSpec(memory_space=pltpu.VMEM),
        scratch_shapes=[pltpu.VMEM((total, 8, 128), jnp.float32)],
        compiler_params=pltpu.CompilerParams(vmem_limit_bytes=32 * 1024 * 1024),
        name="force",
    )(count, far, extended, rho, term)


def passed(value, axis, steps):
    count = lax.axis_size(axis)
    first, last = (max(0, -steps), min(count, count - steps))
    return lax.ppermute(value, axis, [(source, source + steps) for source in range(first, last)])


def extend(block):
    before = passed(block[:, -1:], "gy", 1)
    after = passed(block[:, :1], "gy", -1)
    rows = jnp.concatenate([before, block, after], axis=1)
    return jnp.concatenate([rows, passed(rows[:1], "gx", -1)], axis=0)


def give_back(partial):
    cells_x = partial.shape[0] - 1
    column = passed(partial[cells_x:], "gx", 1)
    summed = partial[:cells_x].at[0:1].add(column)
    from_before = passed(summed[:, -1:], "gy", 1)
    from_after = passed(summed[:, :1], "gy", -1)
    middle = summed[:, 1:-1]
    middle = middle.at[:, :1].add(from_before)
    return middle.at[:, -1:].add(from_after)


def per_device(positions, velocities, counts, cell_pairs, pair_count):
    _, cells_x, cells_y, slots = positions.shape
    cells = (cells_x, cells_y)
    total = (cells_x + 1) * (cells_y + 2)
    codes = cell_pairs.reshape(-1)
    listed = jnp.arange(codes.shape[0], dtype=jnp.int32) < pair_count.reshape(())
    named = jnp.any(
        (codes[:, None] == jnp.arange(cells_x * cells_y * 5, dtype=jnp.int32)[None, :]) & listed[:, None], axis=0
    )
    far = jnp.where(named, 0.0, FAR).astype(jnp.float32)
    occupied = jnp.arange(slots, dtype=jnp.int32)[None, None, :] < counts[:, :, None]
    local = positions - 0.5
    size = jnp.sum(local * local, axis=0) + jnp.where(occupied, 0.0, FAR)
    flow = jnp.sum(local * velocities, axis=0)
    features = jnp.concatenate([local, size[None], velocities, flow[None]], axis=0)
    features = jnp.transpose(features, (1, 2, 0, 3))
    extended = extend(features).reshape(total, 8, slots)
    count = counts.reshape(-1)
    totals = call_density(cells, count, far, extended)
    density = give_back(totals.reshape(cells_x + 1, cells_y + 2, slots))
    density = jnp.where(occupied, density, 0.0)
    rho = extend(density).reshape(total, slots)
    safe_rho = jnp.where(extended[:, 3] < 0.5 * FAR, rho, 1.0)
    safe_rho = jnp.where(safe_rho > 0.0, safe_rho, 1.0)
    term = SOUND_SPEED * SOUND_SPEED * (safe_rho - REST_DENSITY) / (safe_rho * safe_rho)
    forces = call_force(cells, count, far, extended, safe_rho * (1.0 / (VISCOUS * SOUND_SPEED * 2.0 * SMOOTH)), term)
    forces = forces.reshape(cells_x + 1, cells_y + 2, 8, slots)[:, :, :3]
    own = give_back(forces)
    pull = jnp.array([0.0, 0.0, -GRAVITY], dtype=jnp.float32)[:, None, None, None]
    accel = jnp.where(occupied[None], jnp.transpose(own, (2, 0, 1, 3)) + pull, 0.0)
    return density, accel


def solution(mesh):
    placed = (
        P(None, "gx", "gy", None),
        P(None, "gx", "gy", None),
        P("gx", "gy"),
        P("gx", "gy", None),
        P("gx", "gy"),
    )
    return jax.shard_map(
        per_device,
        mesh=mesh,
        in_specs=placed,
        out_specs=(P("gx", "gy", None), P(None, "gx", "gy", None)),
        check_vma=False,
    )
```

time: 896 us -> 332 us (0.37)
  the two profiles are of different devices: /device:TPU:30 before, /device:TPU:20 now
where the time goes in v1:
time: 332 us; the launch traced here: 331 us
  Pallas kernels  216 us (65%)
  starting transfers between devices  84.6 us (25%)
  waiting for transfers between devices  25.3 us (8%)
  other arithmetic  3.44 us (1%)
    pallas_call x1, Pallas kernels, call_force(): pl.pallas_call(functools.partial(force_kernel, cells), out_shape=jax.Shap...  152 us
    ppermute x12, starting transfers between devices, passed(): lax.ppermute(value, axis, [(source, source + steps) for source in range(f...  84.6 us
    pallas_call x1, Pallas kernels, call_density(): pl.pallas_call(functools.partial(density_kernel, cells), out_shape=jax.Sh...  64.1 us
    ppermute x12, waiting for transfers between devices, passed(): lax.ppermute(value, axis, [(source, source + steps) for source in range(f...  25.3 us
  transfers between devices with their start and end apart: 12, of which 8 were waited for; matrix products, arithmetic and copies ran while one was open for 0% of the time, Pallas kernels for 0%

profile of v1, /device:TPU:20, one launch (start us, length us, event | category | flops | bytes accessed | tf_op | source)
XLA Modules:
  0.0 331.3 jit_solution(11994350065020175783)
XLA Ops:
  0.6 0.0 copy-start
  0.6 0.0 copy-start.3
  0.6 1.1 multiply_reduce_fusion.1
  1.8 0.0 copy-start.2
  1.8 0.8 bitcast_add_fusion
  2.6 0.0 copy-done
  2.7 3.8 %collective-permute-start = (f32[4,1,8,128]{3,1,0,2:T(1,128)S(1)}, f32[4,1,8,128]{3,1,0,2:T(1,128)S(1)}, u32[]{:S(2)}, u32[]{:S(2)}) collective-permute-start(f32[4,1,8,128]{3,1,0,2:T(1,128)S(1)} %get-tuple-element.78), channel_id=1, source_target_pairs={{0,1},{1,2},{2,3},{3,4},{4,5},{5,6},{6,7},{7,8},{8,9},{9,10},{10,1... | collective-permute-start | bytes 49160 | tf_op jit(solution)/shard_map/ppermute | solution.py:255
  6.5 11.1 %collective-permute-start.1 = (f32[4,1,8,128]{3,1,0,2:T(1,128)S(1)}, f32[4,1,8,128]{3,1,0,2:T(1,128)S(1)}, u32[]{:S(2)}, u32[]{:S(2)}) collective-permute-start(f32[4,1,8,128]{3,1,0,2:T(1,128)S(1)} %get-tuple-element.79), channel_id=1, source_target_pairs={{1,0},{2,1},{3,2},{4,3},{5,4},{6,5},{7,6},{8,7},{9,8},{10,9},{11,1... | collective-permute-start | bytes 49160 | tf_op jit(solution)/shard_map/ppermute | solution.py:255
  18.3 0.0 copy-done.3
  18.4 0.3 fusion.1
  18.7 0.0 copy-done.2
  18.7 0.1 reshape.242.count_ref
  18.8 0.0 collective-permute-done
  18.8 0.3 collective-permute-done.1
  19.1 12.6 %collective-permute-start.2 = (f32[1,34,8,128]{3,1,0,2:T(8,128)S(1)}, f32[1,34,8,128]{3,1,0,2:T(8,128)S(1)}, u32[]{:S(2)}, u32[]{:S(2)}) collective-permute-start(f32[1,34,8,128]{3,1,0,2:T(8,128)S(1)} %pad_maximum_fusion.1), channel_id=1, source_target_pairs={{32,0},{64,32},{96,64},{128,96},{160,128},{192,160},{224,192},{256... | collective-permute-start | bytes 417800 | tf_op jit(solution)/shard_map/ppermute | solution.py:255
  31.8 2.8 collective-permute-done.2
  34.6 0.1 pad_maximum_fusion
  34.7 0.1 copy.27
  34.8 64.1 %density.1 = f32[170,128]{1,0:T(8,128)S(1)} custom-call(s32[128]{0:T(128)S(1)} %reshape.242.count_ref, f32[640]{0:T(1024)S(1)} %broadcast_select_fusion.1.far_ref, f32[170,8,128]{2,1,0:T(8,128)S(1)} %bitcast.27), custom_call_target="tpu_custom_call" | custom-call | tf_op jit(solution)/shard_map/density/pallas_call | solution.py:224
  98.9 7.3 %collective-permute-start.3 = (f32[1,34,128]{2,1,0:T(8,128)S(1)}, f32[1,34,128]{2,1,0:T(8,128)S(1)}, u32[]{:S(2)}, u32[]{:S(2)}) collective-permute-start(f32[1,34,128]{2,1,0:T(8,128)S(1)} %slice_bitcast_fusion), channel_id=1, source_target_pairs={{0,32},{32,64},{64,96},{96,128},{128,160},{160,192},{192,224},{224... | collective-permute-start | bytes 52232 | tf_op jit(solution)/shard_map/ppermute | solution.py:255
  106.3 7.3 %collective-permute-done.3 = f32[1,34,128]{2,1,0:T(8,128)S(1)} collective-permute-done((f32[1,34,128]{2,1,0:T(8,128)S(1)}, f32[1,34,128]{2,1,0:T(8,128)S(1)}, u32[]{:S(2)}, u32[]{:S(2)}) %collective-permute-start.3) | collective-permute-done | bytes 17440 | tf_op jit(solution)/shard_map/ppermute | solution.py:255
  113.7 1.9 collective-permute-start.4
  115.6 11.9 %collective-permute-start.5 = (f32[4,1,128]{2,1,0:T(1,128)S(1)}, f32[4,1,128]{2,1,0:T(1,128)S(1)}, u32[]{:S(2)}, u32[]{:S(2)}) collective-permute-start(f32[4,1,128]{2,1,0:T(1,128)S(1)} %get-tuple-element.85), channel_id=1, source_target_pairs={{1,0},{2,1},{3,2},{4,3},{5,4},{6,5},{7,6},{8,7},{9,8},{10,9},{11,1... | collective-permute-start | bytes 6152 | tf_op jit(solution)/shard_map/ppermute | solution.py:255
  127.5 0.0 collective-permute-done.4
  127.6 1.2 collective-permute-done.5
  128.8 0.1 broadcast_select_fusion
  128.9 0.0 copy-start.1
  129.0 1.9 collective-permute-start.6
  130.9 11.7 %collective-permute-start.7 = (f32[4,1,128]{2,1,0:T(1,128)S(1)}, f32[4,1,128]{2,1,0:T(1,128)S(1)}, u32[]{:S(2)}, u32[]{:S(2)}) collective-permute-start(f32[4,1,128]{2,1,0:T(1,128)S(1)} %get-tuple-element.88), channel_id=1, source_target_pairs={{1,0},{2,1},{3,2},{4,3},{5,4},{6,5},{7,6},{8,7},{9,8},{10,9},{11,1... | collective-permute-start | bytes 6152 | tf_op jit(solution)/shard_map/ppermute | solution.py:255
  142.6 0.0 collective-permute-done.6
  142.6 1.3 collective-permute-done.7
  143.9 1.9 collective-permute-start.8
  145.8 0.1 slice.259
  145.9 1.4 collective-permute-done.8
  147.3 151.5 %force.1 = f32[170,8,128]{2,1,0:T(8,128)S(1)} custom-call(s32[128]{0:T(128)S(1)} %reshape.242.count_ref, f32[640]{0:T(1024)S(1)} %broadcast_select_fusion.1.far_ref, f32[170,8,128]{2,1,0:T(8,128)S(1)} %bitcast.29, f32[170,128]{1,0:T(8,128)S(1)} %get-tuple-element.84.rho_ref, f32[170,128]{1,0:T(8,128)S(1)} %get-tuple-element.83.term_ref), custom_call_target="tpu_custom_call" | custom-call | tf_op jit(solution)/shard_map/force/pallas_call | solution.py:241
  298.9 0.0 copy-done.1
  298.9 0.0 copy-start.4
  298.9 5.4 %collective-permute-start.9 = (f32[1,34,3,128]{3,1,0,2:T(8,128)S(1)}, f32[1,34,3,128]{3,1,0,2:T(8,128)S(1)}, u32[]{:S(2)}, u32[]{:S(2)}) collective-permute-start(f32[1,34,3,128]{3,1,0,2:T(8,128)S(1)} %copy.35), channel_id=1, source_target_pairs={{0,32},{32,64},{64,96},{96,128},{128,160},{160,192},{192,224},{224... | collective-permute-start | bytes 156680 | tf_op jit(solution)/shard_map/ppermute | solution.py:255
  304.5 9.7 %collective-permute-done.9 = f32[1,34,3,128]{3,1,0,2:T(8,128)S(1)} collective-permute-done((f32[1,34,3,128]{3,1,0,2:T(8,128)S(1)}, f32[1,34,3,128]{3,1,0,2:T(8,128)S(1)}, u32[]{:S(2)}, u32[]{:S(2)}) %collective-permute-start.9) | collective-permute-done | bytes 52256 | tf_op jit(solution)/shard_map/ppermute | solution.py:255
  314.2 1.9 collective-permute-start.10
  316.1 0.1 iota_compare_fusion.2
  316.2 12.9 %collective-permute-start.11 = (f32[4,1,3,128]{3,1,0,2:T(1,128)S(1)}, f32[4,1,3,128]{3,1,0,2:T(1,128)S(1)}, u32[]{:S(2)}, u32[]{:S(2)}) collective-permute-start(f32[4,1,3,128]{3,1,0,2:T(1,128)S(1)} %get-tuple-element.80), channel_id=1, source_target_pairs={{1,0},{2,1},{3,2},{4,3},{5,4},{6,5},{7,6},{8,7},{9,8},{10,9},{11,1... | collective-permute-start | bytes 18440 | tf_op jit(solution)/shard_map/ppermute | solution.py:255
  329.2 0.0 collective-permute-done.10
  329.3 1.2 collective-permute-done.11
  330.6 0.0 copy-done.4
  330.6 0.8 select_bitcast_fusion
  (32 shorter events, 0.5 us)
Async XLA Ops:
  0.6 2.0 copy-start
  0.6 17.7 %copy-start.3 = (s32[1,1,640]{2,1,0:T(1,128)S(1)}, s32[1,1,640]{2,1,0:T(1,128)}, u32[]{:S(2)}) copy-start(s32[1,1,640]{2,1,0:T(1,128)} %param.21) | copy-start | bytes 7684
  1.8 16.9 %copy-start.2 = (s32[4,32]{1,0:T(4,128)S(1)}, s32[4,32]{1,0:T(4,128)}, u32[]{:S(2)}) copy-start(s32[4,32]{1,0:T(4,128)} %param.20) | copy-start | bytes 1540
  2.7 16.1 %collective-permute-start = (f32[4,1,8,128]{3,1,0,2:T(1,128)S(1)}, f32[4,1,8,128]{3,1,0,2:T(1,128)S(1)}, u32[]{:S(2)}, u32[]{:S(2)}) collective-permute-start(f32[4,1,8,128]{3,1,0,2:T(1,128)S(1)} %get-tuple-element.78), channel_id=1, source_target_pairs={{0,1},{1,2},{2,3},{3,4},{4,5},{5,6},{6,7},{7,8},{8,9},{9,10},{10,1... | collective-permute-start | bytes 49160 | tf_op jit(solution)/shard_map/ppermute | solution.py:255
  6.5 12.6 %collective-permute-start.1 = (f32[4,1,8,128]{3,1,0,2:T(1,128)S(1)}, f32[4,1,8,128]{3,1,0,2:T(1,128)S(1)}, u32[]{:S(2)}, u32[]{:S(2)}) collective-permute-start(f32[4,1,8,128]{3,1,0,2:T(1,128)S(1)} %get-tuple-element.79), channel_id=1, source_target_pairs={{1,0},{2,1},{3,2},{4,3},{5,4},{6,5},{7,6},{8,7},{9,8},{10,9},{11,1... | collective-permute-start | bytes 49160 | tf_op jit(solution)/shard_map/ppermute | solution.py:255
  19.1 15.4 %collective-permute-start.2 = (f32[1,34,8,128]{3,1,0,2:T(8,128)S(1)}, f32[1,34,8,128]{3,1,0,2:T(8,128)S(1)}, u32[]{:S(2)}, u32[]{:S(2)}) collective-permute-start(f32[1,34,8,128]{3,1,0,2:T(8,128)S(1)} %pad_maximum_fusion.1), channel_id=1, source_target_pairs={{32,0},{64,32},{96,64},{128,96},{160,128},{192,160},{224,192},{256... | collective-permute-start | bytes 417800 | tf_op jit(solution)/shard_map/ppermute | solution.py:255
  98.9 14.7 %collective-permute-start.3 = (f32[1,34,128]{2,1,0:T(8,128)S(1)}, f32[1,34,128]{2,1,0:T(8,128)S(1)}, u32[]{:S(2)}, u32[]{:S(2)}) collective-permute-start(f32[1,34,128]{2,1,0:T(8,128)S(1)} %slice_bitcast_fusion), channel_id=1, source_target_pairs={{0,32},{32,64},{64,96},{96,128},{128,160},{160,192},{192,224},{224... | collective-permute-start | bytes 52232 | tf_op jit(solution)/shard_map/ppermute | solution.py:255
  113.7 13.9 %collective-permute-start.4 = (f32[4,1,128]{2,1,0:T(1,128)S(1)}, f32[4,1,128]{2,1,0:T(1,128)S(1)}, u32[]{:S(2)}, u32[]{:S(2)}) collective-permute-start(f32[4,1,128]{2,1,0:T(1,128)S(1)} %get-tuple-element.86), channel_id=1, source_target_pairs={{0,1},{1,2},{2,3},{3,4},{4,5},{5,6},{6,7},{7,8},{8,9},{9,10},{10,1... | collective-permute-start | bytes 6152 | tf_op jit(solution)/shard_map/ppermute | solution.py:255
  115.6 13.2 %collective-permute-start.5 = (f32[4,1,128]{2,1,0:T(1,128)S(1)}, f32[4,1,128]{2,1,0:T(1,128)S(1)}, u32[]{:S(2)}, u32[]{:S(2)}) collective-permute-start(f32[4,1,128]{2,1,0:T(1,128)S(1)} %get-tuple-element.85), channel_id=1, source_target_pairs={{1,0},{2,1},{3,2},{4,3},{5,4},{6,5},{7,6},{8,7},{9,8},{10,9},{11,1... | collective-permute-start | bytes 6152 | tf_op jit(solution)/shard_map/ppermute | solution.py:255
  128.9 169.9 %copy-start.1 = (f32[4,32,128]{2,1,0:T(8,128)}, f32[4,32,128]{2,1,0:T(8,128)S(1)}, u32[]{:S(2)}) copy-start(f32[4,32,128]{2,1,0:T(8,128)S(1)} %broadcast_select_fusion) | copy-start | bytes 196612
  129.0 13.6 %collective-permute-start.6 = (f32[4,1,128]{2,1,0:T(1,128)S(1)}, f32[4,1,128]{2,1,0:T(1,128)S(1)}, u32[]{:S(2)}, u32[]{:S(2)}) collective-permute-start(f32[4,1,128]{2,1,0:T(1,128)S(1)} %get-tuple-element.87), channel_id=1, source_target_pairs={{0,1},{1,2},{2,3},{3,4},{4,5},{5,6},{6,7},{7,8},{8,9},{9,10},{10,1... | collective-permute-start | bytes 6152 | tf_op jit(solution)/shard_map/ppermute | solution.py:255
  130.9 13.0 %collective-permute-start.7 = (f32[4,1,128]{2,1,0:T(1,128)S(1)}, f32[4,1,128]{2,1,0:T(1,128)S(1)}, u32[]{:S(2)}, u32[]{:S(2)}) collective-permute-start(f32[4,1,128]{2,1,0:T(1,128)S(1)} %get-tuple-element.88), channel_id=1, source_target_pairs={{1,0},{2,1},{3,2},{4,3},{5,4},{6,5},{7,6},{8,7},{9,8},{10,9},{11,1... | collective-permute-start | bytes 6152 | tf_op jit(solution)/shard_map/ppermute | solution.py:255
  143.9 3.4 %collective-permute-start.8 = (f32[1,34,128]{2,1,0:T(8,128)S(1)}, f32[1,34,128]{2,1,0:T(8,128)S(1)}, u32[]{:S(2)}, u32[]{:S(2)}) collective-permute-start(f32[1,34,128]{2,1,0:T(8,128)S(1)} %pad_maximum_fusion.4), channel_id=1, source_target_pairs={{32,0},{64,32},{96,64},{128,96},{160,128},{192,160},{224,192},{256... | collective-permute-start | bytes 52232 | tf_op jit(solution)/shard_map/ppermute | solution.py:255
  298.9 31.7 %copy-start.4 = (f32[3]{0:T(128)S(1)}, f32[3]{0:T(128)}, u32[]{:S(2)}) copy-start(f32[3]{0:T(128)} %constant.178.clone) | copy-start | bytes 40
  298.9 15.2 %collective-permute-start.9 = (f32[1,34,3,128]{3,1,0,2:T(8,128)S(1)}, f32[1,34,3,128]{3,1,0,2:T(8,128)S(1)}, u32[]{:S(2)}, u32[]{:S(2)}) collective-permute-start(f32[1,34,3,128]{3,1,0,2:T(8,128)S(1)} %copy.35), channel_id=1, source_target_pairs={{0,32},{32,64},{64,96},{96,128},{128,160},{160,192},{192,224},{224... | collective-permute-start | bytes 156680 | tf_op jit(solution)/shard_map/ppermute | solution.py:255
  314.2 15.0 %collective-permute-start.10 = (f32[4,1,3,128]{3,1,0,2:T(1,128)S(1)}, f32[4,1,3,128]{3,1,0,2:T(1,128)S(1)}, u32[]{:S(2)}, u32[]{:S(2)}) collective-permute-start(f32[4,1,3,128]{3,1,0,2:T(1,128)S(1)} %get-tuple-element.81), channel_id=1, source_target_pairs={{0,1},{1,2},{2,3},{3,4},{4,5},{5,6},{6,7},{7,8},{8,9},{9,10},{10,1... | collective-permute-start | bytes 18440 | tf_op jit(solution)/shard_map/ppermute | solution.py:255
  316.2 14.3 %collective-permute-start.11 = (f32[4,1,3,128]{3,1,0,2:T(1,128)S(1)}, f32[4,1,3,128]{3,1,0,2:T(1,128)S(1)}, u32[]{:S(2)}, u32[]{:S(2)}) collective-permute-start(f32[4,1,3,128]{3,1,0,2:T(1,128)S(1)} %get-tuple-element.80), channel_id=1, source_target_pairs={{1,0},{2,1},{3,2},{4,3},{5,4},{6,5},{7,6},{8,7},{9,8},{10,9},{11,1... | collective-permute-start | bytes 18440 | tf_op jit(solution)/shard_map/ppermute | solution.py:255

commit v2 on v1

v2 whole, which is shorter than its diff:
```python
import functools

import jax
import jax.numpy as jnp
from jax import lax
from jax.experimental import pallas as pl
from jax.experimental.pallas import tpu as pltpu
from jax.sharding import PartitionSpec as P

SMOOTH = 0.5
NORMAL = 21.0 / (16.0 * 3.141592653589793 * SMOOTH**3)
PARTICLE_MASS = 1.0 / 128.0
REST_DENSITY = 0.5
SOUND_SPEED = 0.5
VISCOUS = 0.3
GRAVITY = 1.0
STEPS = ((0, 0), (1, 0), (0, 1), (1, 1), (1, -1))
FAR = 1.0e4
TINY = 1.0e-12
GROUP = 16
CLASSES = (8, 7, 6, 5, 4, 3)
TOGETHER = 2
MARGIN = 40
VMEM_BYTES = 56 * 1024 * 1024


def rounded(value):
    return value.astype(jnp.bfloat16).astype(jnp.float32)


def row_ids():
    return lax.broadcasted_iota(jnp.int32, (8, 128), 0)


def at_row(ids, **rows):
    result = jnp.zeros((8, 128), jnp.float32)
    for name, value in rows.items():
        result = jnp.where(ids == int(name[1:]), value, result)
    return result


def partner_block(ids, block, step, far):
    step_x, step_y = step
    size = block[3:4] + far
    if not (step_x or step_y):
        return jnp.where(ids == 3, size, block)
    flow = block[7:8]
    if step_x:
        size = size + 2.0 * step_x * block[0:1]
        flow = flow + float(step_x) * block[4:5]
    if step_y:
        size = size + 2.0 * step_y * block[1:2]
        flow = flow + float(step_y) * block[5:6]
    size = size + float(step_x * step_x + step_y * step_y)
    moved = block + at_row(ids, r0=float(step_x), r1=float(step_y))
    return jnp.where(ids == 3, size, jnp.where(ids == 7, flow, moved))


def right_side(ids, block):
    high = rounded(block)
    rest = block - high
    low = rest - rounded(rest)
    last = jnp.where((ids == 3) | (ids == 7), low, 1.0)
    return jnp.concatenate([high, rest, last, high], axis=0).astype(jnp.bfloat16)


def left_side(ids, form, own):
    high = rounded(form)
    own_high = rounded(own)
    own_rest = own - own_high
    own_middle = rounded(own_rest)
    last = jnp.where((ids == 3) | (ids == 7), form, 0.0)
    last = last + at_row(ids, r0=own_high, r1=own_middle, r2=own_rest - own_middle)
    return [high, high, last, form - high]


def size_form(ids, block):
    return jnp.where(ids < 3, -2.0 * block, jnp.where(ids == 3, 1.0, 0.0)), block[3:4]


def flow_form(ids, block):
    swapped = pltpu.roll(block, 4, 0)
    return jnp.where(ids == 7, -1.0, jnp.where(ids == 3, 0.0, swapped)), -block[7:8]


def split(value):
    high = value.astype(jnp.bfloat16)
    return high, (value - high.astype(jnp.float32)).astype(jnp.bfloat16)


def dot(a, b):
    return jnp.dot(a, b, preferred_element_type=jnp.float32)


def for_pairs(order_ref, start_ref, body):
    for place, group in enumerate(CLASSES):

        @pl.loop(start_ref[place], start_ref[place + 1])
        def _(step, rows=group * GROUP):
            body([order_ref[TOGETHER * step + turn] for turn in range(TOGETHER)], rows)


def home_of(cell, cells_y):
    return cell // cells_y * (cells_y + 2) + cell % cells_y + 1


def density_kernel(cells, order_ref, start_ref, far_ref, p_ref, out_ref, left_ref, right_ref, part_ref, total_ref):
    cells_x, cells_y = cells
    span = cells_y + 2
    ids = row_ids()
    part_ref[...] = jnp.zeros_like(part_ref)

    @pl.loop(0, cells_x * cells_y)
    def _(cell):
        home = home_of(cell, cells_y)
        left = left_side(ids, *size_form(ids, p_ref[home]))
        left_ref[cell] = jnp.concatenate(left, axis=0).T.astype(jnp.bfloat16)
        for kind, (step_x, step_y) in enumerate(STEPS):
            block = p_ref[home + step_x * span + step_y]
            partner = partner_block(ids, block, (step_x, step_y), far_ref[cell * 5 + kind])
            right_ref[cell * 5 + kind] = right_side(ids, partner)

    def body(chosen, rows):
        for cell in chosen:
            left = left_ref[cell, :rows]
            home = home_of(cell, cells_y) + MARGIN
            total = None
            for kinds in ((0, 1), (2, 3), (4,)):
                squares = dot(left, jnp.concatenate([right_ref[cell * 5 + kind] for kind in kinds], axis=1))
                for turn, kind in enumerate(kinds):
                    safe = jnp.maximum(squares[:, 128 * turn : 128 * turn + 128], TINY)
                    near = jnp.maximum(1.0 - safe * lax.rsqrt(safe), 0.0)
                    two = near * near
                    weight = two * two * (5.0 - 4.0 * near)
                    part_ref[kind, home] = jnp.sum(weight.reshape(rows // 8, 8, 128), axis=0)
                    if kind:
                        total = weight if total is None else total + weight
            total_ref[cell, :rows] = total

    for_pairs(order_ref, start_ref, body)

    @pl.loop(0, cells_x * cells_y // 2)
    def _(pair):
        for turn in range(2):
            cell = 2 * pair + turn
            turned = total_ref[cell].T
            home = home_of(cell, cells_y) + MARGIN
            part_ref[0, home] += jnp.sum(turned.reshape(16, 8, 128), axis=0)

    @pl.loop(0, out_ref.shape[0] // 8)
    def _(block):
        sums = gathered(part_ref, block, span)
        first = pl.multiple_of(block * 8, 8)
        out_ref[pl.ds(first, 8)] = (PARTICLE_MASS * NORMAL) * jnp.sum(sums, axis=1)


def gathered(part_ref, block, span):
    sums = None
    for kind, (step_x, step_y) in enumerate(STEPS):
        piece = part_ref[kind, pl.ds(MARGIN + block * 8 - step_x * span - step_y, 8)]
        sums = piece if sums is None else sums + piece
    return sums


def force_kernel(
    cells, order_ref, start_ref, far_ref, p_ref, rho_ref, term_ref, out_ref,
    left_ref, right_ref, side_ref, place_ref, turned_ref, part_ref, total_ref,
):
    cells_x, cells_y = cells
    span = cells_y + 2
    ids = row_ids()
    part_ref[...] = jnp.zeros_like(part_ref)

    def base_of(home):
        row = (home // span).astype(jnp.float32)
        col = (home % span).astype(jnp.float32)
        return at_row(ids, r0=row, r1=col)

    @pl.loop(0, cells_x * cells_y)
    def _(cell):
        home = home_of(cell, cells_y)
        block = p_ref[home]
        blocks = left_side(ids, *size_form(ids, block)) + left_side(ids, *flow_form(ids, block))
        left_ref[cell] = jnp.concatenate(blocks, axis=0).T.astype(jnp.bfloat16)
        side_ref[cell] = at_row(ids, r0=rho_ref[pl.ds(home, 1)], r1=term_ref[pl.ds(home, 1)]).T
        here = jnp.where(ids < 3, block, jnp.where(ids == 3, 1.0, 0.0))
        high = rounded(here)
        place_ref[cell] = jnp.concatenate([high, here - high], axis=0).astype(jnp.bfloat16)
        for kind, (step_x, step_y) in enumerate(STEPS):
            block = p_ref[home + step_x * span + step_y]
            partner = partner_block(ids, block, (step_x, step_y), far_ref[cell * 5 + kind])
            right_ref[cell * 5 + kind] = right_side(ids, partner)

    @pl.loop(0, (cells_x + 1) * span // 2)
    def _(pair):
        for turn in range(2):
            home = 2 * pair + turn
            here = jnp.where(ids < 3, p_ref[home] + base_of(home), jnp.where(ids == 3, 1.0, 0.0))
            high = rounded(here)
            rest = here - high
            middle = rounded(rest)
            zeros = jnp.zeros((8, 128), jnp.float32)
            stacked = jnp.concatenate([high, middle, rest - middle, zeros], axis=0)
            turned_ref[home] = stacked.T.astype(jnp.bfloat16)

    def body(chosen, rows):
        empty = jnp.zeros((32, 128), jnp.bfloat16)
        for cell in chosen:
            left = left_ref[cell, :rows]
            own = place_ref[cell]
            home = home_of(cell, cells_y)
            rho_i = jnp.broadcast_to(side_ref[cell, :rows, 0:1], (rows, 128))
            term_i = jnp.broadcast_to(side_ref[cell, :rows, 1:2], (rows, 128))
            highs, lows, places = [], [], []
            for kind, (step_x, step_y) in enumerate(STEPS):
                other = home + step_x * span + step_y
                side = right_ref[cell * 5 + kind]
                upper = jnp.concatenate([side, empty], axis=1)
                lower = jnp.concatenate([empty, side], axis=1)
                forms = dot(left, jnp.concatenate([upper, lower], axis=0))
                safe = jnp.maximum(forms[:, :128], TINY)
                near = jnp.maximum(1.0 - safe * lax.rsqrt(safe), 0.0)
                cubed = near * near * near
                bottom = (safe + 0.01 * SMOOTH * SMOOTH) * (rho_i + rho_ref[pl.ds(other, 1)])
                damping = jnp.maximum(forms[:, 128:], 0.0) * pl.reciprocal(bottom, approx=True)
                scalar = (term_i + term_ref[pl.ds(other, 1)] + damping) * cubed
                high, low = split(scalar)
                column = dot(own[:, :rows], high) + dot(own[:, :rows], low)
                column = column[:8] + column[8:]
                if kind:
                    column = column - at_row(ids, r0=float(step_x), r1=float(step_y)) * column[3:4]
                    highs.append(high)
                    lows.append(low)
                    places.append(turned_ref[other])
                part_ref[kind, home + MARGIN] = column
            streams = jnp.concatenate(
                [jnp.concatenate(highs, axis=1), jnp.concatenate(lows, axis=1)], axis=0
            )
            sums = dot(streams, jnp.concatenate(places, axis=0))
            total_ref[cell, :rows] = sums[:rows] + sums[rows:]

    for_pairs(order_ref, start_ref, body)

    @pl.loop(0, cells_x * cells_y // 2)
    def _(pair):
        for turn in range(2):
            cell = 2 * pair + turn
            home = home_of(cell, cells_y)
            sums = total_ref[cell].T
            sums = sums[0:8] + sums[8:16] + sums[16:24]
            part_ref[0, home + MARGIN] += sums - base_of(home) * sums[3:4]

    scale = PARTICLE_MASS * 5.0 * NORMAL / (SMOOTH * SMOOTH)

    @pl.loop(0, out_ref.shape[0] // 8)
    def _(block):
        sums = gathered(part_ref, block, span)
        first = pl.multiple_of(block * 8, 8)
        here = p_ref[pl.ds(first, 8)]
        out_ref[pl.ds(first, 8)] = scale * (here * sums[:, 3:4] - sums)


def padded(total):
    return (total + 7) // 8 * 8


def call_density(cells, order, start, far, extended):
    own, total = cells[0] * cells[1], extended.shape[0]
    return pl.pallas_call(
        functools.partial(density_kernel, cells),
        out_shape=jax.ShapeDtypeStruct((total, 128), jnp.float32),
        in_specs=[pl.BlockSpec(memory_space=pltpu.SMEM)] * 3 + [pl.BlockSpec(memory_space=pltpu.VMEM)],
        out_specs=pl.BlockSpec(memory_space=pltpu.VMEM),
        scratch_shapes=[
            pltpu.VMEM((own, 128, 32), jnp.bfloat16),
            pltpu.VMEM((own * 5, 32, 128), jnp.bfloat16),
            pltpu.VMEM((5, total + MARGIN, 8, 128), jnp.float32),
            pltpu.VMEM((own, 128, 128), jnp.float32),
        ],
        compiler_params=pltpu.CompilerParams(vmem_limit_bytes=VMEM_BYTES),
        name="density",
    )(order, start, far, extended)


def call_force(cells, order, start, far, extended, rho, term):
    own, total = cells[0] * cells[1], extended.shape[0]
    return pl.pallas_call(
        functools.partial(force_kernel, cells),
        out_shape=jax.ShapeDtypeStruct((total, 8, 128), jnp.float32),
        in_specs=[pl.BlockSpec(memory_space=pltpu.SMEM)] * 3 + [pl.BlockSpec(memory_space=pltpu.VMEM)] * 3,
        out_specs=pl.BlockSpec(memory_space=pltpu.VMEM),
        scratch_shapes=[
            pltpu.VMEM((own, 128, 64), jnp.bfloat16),
            pltpu.VMEM((own * 5, 32, 128), jnp.bfloat16),
            pltpu.VMEM((own, 128, 8), jnp.float32),
            pltpu.VMEM((own, 16, 128), jnp.bfloat16),
            pltpu.VMEM((total, 128, 32), jnp.bfloat16),
            pltpu.VMEM((5, total + MARGIN, 8, 128), jnp.float32),
            pltpu.VMEM((own, 128, 32), jnp.float32),
        ],
        compiler_params=pltpu.CompilerParams(vmem_limit_bytes=VMEM_BYTES),
        name="force",
    )(order, start, far, extended, rho, term)


def passed(value, axis, steps):
    count = lax.axis_size(axis)
    first, last = (max(0, -steps), min(count, count - steps))
    return lax.ppermute(value, axis, [(source, source + steps) for source in range(first, last)])


def extend(block):
    before = passed(block[:, -1:], "gy", 1)
    after = passed(block[:, :1], "gy", -1)
    rows = jnp.concatenate([before, block, after], axis=1)
    return jnp.concatenate([rows, passed(rows[:1], "gx", -1)], axis=0)


def give_back(partial):
    cells_x = partial.shape[0] - 1
    column = passed(partial[cells_x:], "gx", 1)
    summed = partial[:cells_x].at[0:1].add(column)
    from_before = passed(summed[:, -1:], "gy", 1)
    from_after = passed(summed[:, :1], "gy", -1)
    middle = summed[:, 1:-1]
    middle = middle.at[:, :1].add(from_before)
    return middle.at[:, -1:].add(from_after)


def row_classes(count):
    cells = count.shape[0]
    group = jnp.clip((count + GROUP - 1) // GROUP, CLASSES[-1], CLASSES[0])
    index = jnp.arange(cells, dtype=jnp.int32)
    ahead = (group[None, :] > group[:, None]) | ((group[None, :] == group[:, None]) & (index[None, :] < index[:, None]))
    rank = jnp.sum(ahead.astype(jnp.int32), axis=1)
    order = jnp.sum(jnp.where(rank[:, None] == index[None, :], index[:, None], 0), axis=0)
    bounds = jnp.array((CLASSES[0] + 1,) + CLASSES, dtype=jnp.int32)
    reached = jnp.sum((group[None, :] >= bounds[:, None]).astype(jnp.int32), axis=1)
    return order, (reached + TOGETHER - 1) // TOGETHER


def per_device(positions, velocities, counts, cell_pairs, pair_count):
    _, cells_x, cells_y, slots = positions.shape
    cells = (cells_x, cells_y)
    total = (cells_x + 1) * (cells_y + 2)
    codes = cell_pairs.reshape(-1)
    listed = jnp.arange(codes.shape[0], dtype=jnp.int32) < pair_count.reshape(())
    named = jnp.any(
        (codes[:, None] == jnp.arange(cells_x * cells_y * 5, dtype=jnp.int32)[None, :]) & listed[:, None], axis=0
    )
    far = jnp.where(named, 0.0, FAR).astype(jnp.float32)
    occupied = jnp.arange(slots, dtype=jnp.int32)[None, None, :] < counts[:, :, None]
    local = positions - 0.5
    size = jnp.sum(local * local, axis=0) + jnp.where(occupied, 0.0, FAR)
    flow = jnp.sum(local * velocities, axis=0)
    features = jnp.concatenate([local, size[None], velocities, flow[None]], axis=0)
    features = jnp.transpose(features, (1, 2, 0, 3))
    extended = extend(features).reshape(total, 8, slots)
    extended = jnp.pad(extended, ((0, padded(total) - total), (0, 0), (0, 0)))
    order, start = row_classes(counts.reshape(-1))
    totals = call_density(cells, order, start, far, extended)
    density = give_back(totals[:total].reshape(cells_x + 1, cells_y + 2, slots))
    density = jnp.where(occupied, density, 0.0)
    rho = extend(density).reshape(total, slots)
    rho = jnp.pad(rho, ((0, padded(total) - total), (0, 0)))
    safe_rho = jnp.where(extended[:, 3] < 0.5 * FAR, rho, 1.0)
    safe_rho = jnp.where(safe_rho > 0.0, safe_rho, 1.0)
    term = SOUND_SPEED * SOUND_SPEED * (safe_rho - REST_DENSITY) / (safe_rho * safe_rho)
    forces = call_force(
        cells, order, start, far, extended, safe_rho * (1.0 / (VISCOUS * SOUND_SPEED * 2.0 * SMOOTH)), term
    )
    forces = forces[:total].reshape(cells_x + 1, cells_y + 2, 8, slots)[:, :, :3]
    own = give_back(forces)
    pull = jnp.array([0.0, 0.0, -GRAVITY], dtype=jnp.float32)[:, None, None, None]
    accel = jnp.where(occupied[None], jnp.transpose(own, (2, 0, 1, 3)) + pull, 0.0)
    return density, accel


def solution(mesh):
    placed = (
        P(None, "gx", "gy", None),
        P(None, "gx", "gy", None),
        P("gx", "gy"),
        P("gx", "gy", None),
        P("gx", "gy"),
    )
    return jax.shard_map(
        per_device,
        mesh=mesh,
        in_specs=placed,
        out_specs=(P("gx", "gy", None), P(None, "gx", "gy", None)),
        check_vma=False,
    )
```

time: 332 us -> 251 us (0.76)
  the two profiles are of different devices: /device:TPU:20 before, /device:TPU:30 now
where the time goes in v2:
time: 251 us; the launch traced here: 250 us
  Pallas kernels  130 us (52%)
  starting transfers between devices  79.7 us (32%)
  waiting for transfers between devices  27.3 us (11%)
  other arithmetic  6.98 us (3%)
  local copies, waits for them, and re-layouts  4.62 us (2%)
    pallas_call x1, Pallas kernels, call_force(): pl.pallas_call(functools.partial(force_kernel, cells), out_shape=jax.Shap...  84.6 us
    ppermute x12, starting transfers between devices, passed(): lax.ppermute(value, axis, [(source, source + steps) for source in range(f...  79.7 us
    pallas_call x1, Pallas kernels, call_density(): pl.pallas_call(functools.partial(density_kernel, cells), out_shape=jax.Sh...  45.6 us
    ppermute x12, waiting for transfers between devices, passed(): lax.ppermute(value, axis, [(source, source + steps) for source in range(f...  27.3 us
  transfers between devices with their start and end apart: 12, of which 7 were waited for; matrix products, arithmetic and copies ran while one was open for 1% of the time, Pallas kernels for 0%

profile of v2, /device:TPU:30, one launch (start us, length us, event | category | flops | bytes accessed | tf_op | source)
XLA Modules:
  0.0 250.4 jit_solution(13496120968439480909)
XLA Ops:
  0.6 0.0 copy-start.2
  0.7 1.2 multiply_reduce_fusion.1
  1.8 0.0 copy-start.5
  1.8 0.8 bitcast_add_fusion
  2.7 3.8 %collective-permute-start = (f32[4,1,8,128]{3,1,0,2:T(1,128)S(1)}, f32[4,1,8,128]{3,1,0,2:T(1,128)S(1)}, u32[]{:S(2)}, u32[]{:S(2)}) collective-permute-start(f32[4,1,8,128]{3,1,0,2:T(1,128)S(1)} %get-tuple-element.80), channel_id=1, source_target_pairs={{0,1},{1,2},{2,3},{3,4},{4,5},{5,6},{6,7},{7,8},{8,9},{9,10},{10,1... | collective-permute-start | bytes 49160 | tf_op jit(solution)/shard_map/ppermute | solution.py:309
  6.5 11.4 %collective-permute-start.1 = (f32[4,1,8,128]{3,1,0,2:T(1,128)S(1)}, f32[4,1,8,128]{3,1,0,2:T(1,128)S(1)}, u32[]{:S(2)}, u32[]{:S(2)}) collective-permute-start(f32[4,1,8,128]{3,1,0,2:T(1,128)S(1)} %get-tuple-element.81), channel_id=1, source_target_pairs={{1,0},{2,1},{3,2},{4,3},{5,4},{6,5},{7,6},{8,7},{9,8},{10,9},{11,1... | collective-permute-start | bytes 49160 | tf_op jit(solution)/shard_map/ppermute | solution.py:309
  18.0 0.1 sub.35
  18.8 0.3 fusion.1
  19.1 0.6 broadcast_select_fusion.1.far_ref
  19.7 0.2 convert_reduce_fusion.1
  19.9 0.6 and_select_fusion.start_ref
  20.5 13.0 %collective-permute-start.2 = (f32[1,34,8,128]{3,1,0,2:T(8,128)S(1)}, f32[1,34,8,128]{3,1,0,2:T(8,128)S(1)}, u32[]{:S(2)}, u32[]{:S(2)}) collective-permute-start(f32[1,34,8,128]{3,1,0,2:T(8,128)S(1)} %pad_maximum_fusion.1), channel_id=1, source_target_pairs={{32,0},{64,32},{96,64},{128,96},{160,128},{192,160},{224,192},{256... | collective-permute-start | bytes 417800 | tf_op jit(solution)/shard_map/ppermute | solution.py:309
  33.5 0.2 convert_reduce_fusion
  33.6 0.6 select_reduce_fusion.order_ref
  34.2 2.0 collective-permute-done.2
  36.3 0.1 pad_maximum_fusion
  36.4 0.1 copy.32
  36.5 0.1 copy.33
  36.7 0.2 copy.45
  36.9 0.9 pad.20.clone.p_ref
  37.8 45.6 %density.1 = f32[176,128]{1,0:T(8,128)} custom-call(s32[128]{0:T(128)} %select_reduce_fusion.order_ref, s32[7]{0:T(128)} %and_select_fusion.start_ref, f32[640]{0:T(1024)} %broadcast_select_fusion.1.far_ref, f32[176,8,128]{2,1,0:T(8,128)} %pad.20.clone.p_ref), custom_call_target="tpu_custom_call" | custom-call | tf_op jit(solution)/shard_map/density/pallas_call | solution.py:269
  83.4 0.7 slice_bitcast_fusion
  84.1 5.6 %collective-permute-start.3 = (f32[1,34,128]{2,1,0:T(8,128)S(1)}, f32[1,34,128]{2,1,0:T(8,128)S(1)}, u32[]{:S(2)}, u32[]{:S(2)}) collective-permute-start(f32[1,34,128]{2,1,0:T(8,128)S(1)} %slice_bitcast_fusion), channel_id=1, source_target_pairs={{0,32},{32,64},{64,96},{96,128},{128,160},{160,192},{192,224},{224... | collective-permute-start | bytes 52232 | tf_op jit(solution)/shard_map/ppermute | solution.py:309
  89.7 0.9 slice.258
  90.6 8.2 %collective-permute-done.3 = f32[1,34,128]{2,1,0:T(8,128)S(1)} collective-permute-done((f32[1,34,128]{2,1,0:T(8,128)S(1)}, f32[1,34,128]{2,1,0:T(8,128)S(1)}, u32[]{:S(2)}, u32[]{:S(2)}) %collective-permute-start.3) | collective-permute-done | bytes 17440 | tf_op jit(solution)/shard_map/ppermute | solution.py:309
  98.8 0.7 fusion.7
  99.5 1.9 collective-permute-start.4
  101.5 11.4 %collective-permute-start.5 = (f32[4,1,128]{2,1,0:T(1,128)S(1)}, f32[4,1,128]{2,1,0:T(1,128)S(1)}, u32[]{:S(2)}, u32[]{:S(2)}) collective-permute-start(f32[4,1,128]{2,1,0:T(1,128)S(1)} %get-tuple-element.85), channel_id=1, source_target_pairs={{1,0},{2,1},{3,2},{4,3},{5,4},{6,5},{7,6},{8,7},{9,8},{10,9},{11,1... | collective-permute-start | bytes 6152 | tf_op jit(solution)/shard_map/ppermute | solution.py:309
  112.9 0.0 collective-permute-done.4
  113.0 1.2 collective-permute-done.5
  114.2 0.1 broadcast_select_fusion
  114.3 0.0 copy-start.1
  114.3 1.9 collective-permute-start.6
  116.3 11.7 %collective-permute-start.7 = (f32[4,1,128]{2,1,0:T(1,128)S(1)}, f32[4,1,128]{2,1,0:T(1,128)S(1)}, u32[]{:S(2)}, u32[]{:S(2)}) collective-permute-start(f32[4,1,128]{2,1,0:T(1,128)S(1)} %get-tuple-element.88), channel_id=1, source_target_pairs={{1,0},{2,1},{3,2},{4,3},{5,4},{6,5},{7,6},{8,7},{9,8},{10,9},{11,1... | collective-permute-start | bytes 6152 | tf_op jit(solution)/shard_map/ppermute | solution.py:309
  128.0 1.3 collective-permute-done.7
  129.3 1.9 collective-permute-start.8
  131.2 1.5 collective-permute-done.8
  132.7 0.7 multiply_divide_fusion
  133.4 84.6 %force.1 = f32[176,8,128]{2,1,0:T(8,128)} custom-call(s32[128]{0:T(128)} %select_reduce_fusion.order_ref, s32[7]{0:T(128)} %and_select_fusion.start_ref, f32[640]{0:T(1024)} %broadcast_select_fusion.1.far_ref, f32[176,8,128]{2,1,0:T(8,128)} %pad.20.clone.p_ref, f32[176,128]{1,0:T(8,128)} %get-tuple-element.77.rho_ref, f32[176,128]{1,0:T(8,128)} %get-tuple-element.76.term_ref), custom_call_target="tpu_custom_call" | custom-call | tf_op jit(solution)/shard_map/force/pallas_call | solution.py:287
  218.0 1.1 slice.268
  219.1 0.0 copy-start.4
  219.2 3.6 %collective-permute-start.9 = (f32[1,34,3,128]{3,1,0,2:T(8,128)S(1)}, f32[1,34,3,128]{3,1,0,2:T(8,128)S(1)}, u32[]{:S(2)}, u32[]{:S(2)}) collective-permute-start(f32[1,34,3,128]{3,1,0,2:T(8,128)S(1)} %copy.41), channel_id=1, source_target_pairs={{0,32},{32,64},{64,96},{96,128},{128,160},{160,192},{192,224},{224... | collective-permute-start | bytes 156680 | tf_op jit(solution)/shard_map/ppermute | solution.py:309
  222.8 11.8 %collective-permute-done.9 = f32[1,34,3,128]{3,1,0,2:T(8,128)S(1)} collective-permute-done((f32[1,34,3,128]{3,1,0,2:T(8,128)S(1)}, f32[1,34,3,128]{3,1,0,2:T(8,128)S(1)}, u32[]{:S(2)}, u32[]{:S(2)}) %collective-permute-start.9) | collective-permute-done | bytes 52256 | tf_op jit(solution)/shard_map/ppermute | solution.py:309
  234.6 1.9 collective-permute-start.10
  236.6 0.1 iota_compare_fusion.4
  236.7 11.6 %collective-permute-start.11 = (f32[4,1,3,128]{3,1,0,2:T(1,128)S(1)}, f32[4,1,3,128]{3,1,0,2:T(1,128)S(1)}, u32[]{:S(2)}, u32[]{:S(2)}) collective-permute-start(f32[4,1,3,128]{3,1,0,2:T(1,128)S(1)} %get-tuple-element.82), channel_id=1, source_target_pairs={{1,0},{2,1},{3,2},{4,3},{5,4},{6,5},{7,6},{8,7},{9,8},{10,9},{11,1... | collective-permute-start | bytes 18440 | tf_op jit(solution)/shard_map/ppermute | solution.py:309
  248.3 1.2 collective-permute-done.11
  249.7 0.8 select_bitcast_fusion
  (41 shorter events, 0.5 us)
Async XLA Ops:
  0.6 2.0 copy-start
  0.6 17.3 %copy-start.2 = (s32[4,32]{1,0:T(4,128)S(1)}, s32[4,32]{1,0:T(4,128)}, u32[]{:S(2)}) copy-start(s32[4,32]{1,0:T(4,128)} %param.21) | copy-start | bytes 1540
  0.7 18.1 %copy-start.3 = (s32[1,1,640]{2,1,0:T(1,128)S(1)}, s32[1,1,640]{2,1,0:T(1,128)}, u32[]{:S(2)}) copy-start(s32[1,1,640]{2,1,0:T(1,128)} %param.22) | copy-start | bytes 7684
  1.8 17.9 %copy-start.5 = (s32[7]{0:T(128)S(1)}, s32[7]{0:T(128)}, u32[]{:S(2)}) copy-start(s32[7]{0:T(128)} %constant.221.clone) | copy-start | bytes 88
  2.7 17.8 %collective-permute-start = (f32[4,1,8,128]{3,1,0,2:T(1,128)S(1)}, f32[4,1,8,128]{3,1,0,2:T(1,128)S(1)}, u32[]{:S(2)}, u32[]{:S(2)}) collective-permute-start(f32[4,1,8,128]{3,1,0,2:T(1,128)S(1)} %get-tuple-element.80), channel_id=1, source_target_pairs={{0,1},{1,2},{2,3},{3,4},{4,5},{5,6},{6,7},{7,8},{8,9},{9,10},{10,1... | collective-permute-start | bytes 49160 | tf_op jit(solution)/shard_map/ppermute | solution.py:309
  6.5 14.0 %collective-permute-start.1 = (f32[4,1,8,128]{3,1,0,2:T(1,128)S(1)}, f32[4,1,8,128]{3,1,0,2:T(1,128)S(1)}, u32[]{:S(2)}, u32[]{:S(2)}) collective-permute-start(f32[4,1,8,128]{3,1,0,2:T(1,128)S(1)} %get-tuple-element.81), channel_id=1, source_target_pairs={{1,0},{2,1},{3,2},{4,3},{5,4},{6,5},{7,6},{8,7},{9,8},{10,9},{11,1... | collective-permute-start | bytes 49160 | tf_op jit(solution)/shard_map/ppermute | solution.py:309
  20.5 15.8 %collective-permute-start.2 = (f32[1,34,8,128]{3,1,0,2:T(8,128)S(1)}, f32[1,34,8,128]{3,1,0,2:T(8,128)S(1)}, u32[]{:S(2)}, u32[]{:S(2)}) collective-permute-start(f32[1,34,8,128]{3,1,0,2:T(8,128)S(1)} %pad_maximum_fusion.1), channel_id=1, source_target_pairs={{32,0},{64,32},{96,64},{128,96},{160,128},{192,160},{224,192},{256... | collective-permute-start | bytes 417800 | tf_op jit(solution)/shard_map/ppermute | solution.py:309
  84.1 14.7 %collective-permute-start.3 = (f32[1,34,128]{2,1,0:T(8,128)S(1)}, f32[1,34,128]{2,1,0:T(8,128)S(1)}, u32[]{:S(2)}, u32[]{:S(2)}) collective-permute-start(f32[1,34,128]{2,1,0:T(8,128)S(1)} %slice_bitcast_fusion), channel_id=1, source_target_pairs={{0,32},{32,64},{64,96},{96,128},{128,160},{160,192},{192,224},{224... | collective-permute-start | bytes 52232 | tf_op jit(solution)/shard_map/ppermute | solution.py:309
  99.5 13.4 %collective-permute-start.4 = (f32[4,1,128]{2,1,0:T(1,128)S(1)}, f32[4,1,128]{2,1,0:T(1,128)S(1)}, u32[]{:S(2)}, u32[]{:S(2)}) collective-permute-start(f32[4,1,128]{2,1,0:T(1,128)S(1)} %get-tuple-element.86), channel_id=1, source_target_pairs={{0,1},{1,2},{2,3},{3,4},{4,5},{5,6},{6,7},{7,8},{8,9},{9,10},{10,1... | collective-permute-start | bytes 6152 | tf_op jit(solution)/shard_map/ppermute | solution.py:309
  101.5 12.7 %collective-permute-start.5 = (f32[4,1,128]{2,1,0:T(1,128)S(1)}, f32[4,1,128]{2,1,0:T(1,128)S(1)}, u32[]{:S(2)}, u32[]{:S(2)}) collective-permute-start(f32[4,1,128]{2,1,0:T(1,128)S(1)} %get-tuple-element.85), channel_id=1, source_target_pairs={{1,0},{2,1},{3,2},{4,3},{5,4},{6,5},{7,6},{8,7},{9,8},{10,9},{11,1... | collective-permute-start | bytes 6152 | tf_op jit(solution)/shard_map/ppermute | solution.py:309
  114.3 103.6 %copy-start.1 = (f32[4,32,128]{2,1,0:T(8,128)}, f32[4,32,128]{2,1,0:T(8,128)S(1)}, u32[]{:S(2)}) copy-start(f32[4,32,128]{2,1,0:T(8,128)S(1)} %broadcast_select_fusion) | copy-start | bytes 196612
  114.3 13.6 %collective-permute-start.6 = (f32[4,1,128]{2,1,0:T(1,128)S(1)}, f32[4,1,128]{2,1,0:T(1,128)S(1)}, u32[]{:S(2)}, u32[]{:S(2)}) collective-permute-start(f32[4,1,128]{2,1,0:T(1,128)S(1)} %get-tuple-element.87), channel_id=1, source_target_pairs={{0,1},{1,2},{2,3},{3,4},{4,5},{5,6},{6,7},{7,8},{8,9},{9,10},{10,1... | collective-permute-start | bytes 6152 | tf_op jit(solution)/shard_map/ppermute | solution.py:309
  116.3 13.0 %collective-permute-start.7 = (f32[4,1,128]{2,1,0:T(1,128)S(1)}, f32[4,1,128]{2,1,0:T(1,128)S(1)}, u32[]{:S(2)}, u32[]{:S(2)}) collective-permute-start(f32[4,1,128]{2,1,0:T(1,128)S(1)} %get-tuple-element.88), channel_id=1, source_target_pairs={{1,0},{2,1},{3,2},{4,3},{5,4},{6,5},{7,6},{8,7},{9,8},{10,9},{11,1... | collective-permute-start | bytes 6152 | tf_op jit(solution)/shard_map/ppermute | solution.py:309
  129.3 3.4 %collective-permute-start.8 = (f32[1,34,128]{2,1,0:T(8,128)S(1)}, f32[1,34,128]{2,1,0:T(8,128)S(1)}, u32[]{:S(2)}, u32[]{:S(2)}) collective-permute-start(f32[1,34,128]{2,1,0:T(8,128)S(1)} %pad_maximum_fusion.4), channel_id=1, source_target_pairs={{32,0},{64,32},{96,64},{128,96},{160,128},{192,160},{224,192},{256... | collective-permute-start | bytes 52232 | tf_op jit(solution)/shard_map/ppermute | solution.py:309
  219.1 30.5 %copy-start.4 = (f32[3]{0:T(128)S(1)}, f32[3]{0:T(128)}, u32[]{:S(2)}) copy-start(f32[3]{0:T(128)} %constant.222.clone) | copy-start | bytes 40
  219.2 15.4 %collective-permute-start.9 = (f32[1,34,3,128]{3,1,0,2:T(8,128)S(1)}, f32[1,34,3,128]{3,1,0,2:T(8,128)S(1)}, u32[]{:S(2)}, u32[]{:S(2)}) collective-permute-start(f32[1,34,3,128]{3,1,0,2:T(8,128)S(1)} %copy.41), channel_id=1, source_target_pairs={{0,32},{32,64},{64,96},{96,128},{128,160},{160,192},{192,224},{224... | collective-permute-start | bytes 156680 | tf_op jit(solution)/shard_map/ppermute | solution.py:309
  234.6 13.6 %collective-permute-start.10 = (f32[4,1,3,128]{3,1,0,2:T(1,128)S(1)}, f32[4,1,3,128]{3,1,0,2:T(1,128)S(1)}, u32[]{:S(2)}, u32[]{:S(2)}) collective-permute-start(f32[4,1,3,128]{3,1,0,2:T(1,128)S(1)} %get-tuple-element.83), channel_id=1, source_target_pairs={{0,1},{1,2},{2,3},{3,4},{4,5},{5,6},{6,7},{7,8},{8,9},{9,10},{10,1... | collective-permute-start | bytes 18440 | tf_op jit(solution)/shard_map/ppermute | solution.py:309
  236.7 12.9 %collective-permute-start.11 = (f32[4,1,3,128]{3,1,0,2:T(1,128)S(1)}, f32[4,1,3,128]{3,1,0,2:T(1,128)S(1)}, u32[]{:S(2)}, u32[]{:S(2)}) collective-permute-start(f32[4,1,3,128]{3,1,0,2:T(1,128)S(1)} %get-tuple-element.82), channel_id=1, source_target_pairs={{1,0},{2,1},{3,2},{4,3},{5,4},{6,5},{7,6},{8,7},{9,8},{10,9},{11,1... | collective-permute-start | bytes 18440 | tf_op jit(solution)/shard_map/ppermute | solution.py:309

commit v3 on v2

v3 whole, which is shorter than its diff:
```python
import functools

import jax
import jax.numpy as jnp
from jax import lax
from jax.experimental import pallas as pl
from jax.experimental.pallas import tpu as pltpu
from jax.sharding import PartitionSpec as P

SMOOTH = 0.5
NORMAL = 21.0 / (16.0 * 3.141592653589793 * SMOOTH**3)
PARTICLE_MASS = 1.0 / 128.0
REST_DENSITY = 0.5
SOUND_SPEED = 0.5
VISCOUS = 0.3
GRAVITY = 1.0
STEPS = ((0, 0), (1, 0), (0, 1), (1, 1), (1, -1))
FAR = 1.0e4
TINY = 1.0e-12
MARGIN = 40
VMEM_BYTES = 56 * 1024 * 1024
MESH = pl.DeviceIdType.MESH


def rounded(value):
    return value.astype(jnp.bfloat16).astype(jnp.float32)


def row_ids():
    return lax.broadcasted_iota(jnp.int32, (8, 128), 0)


def at_row(ids, **rows):
    result = jnp.zeros((8, 128), jnp.float32)
    for name, value in rows.items():
        result = jnp.where(ids == int(name[1:]), value, result)
    return result


def partner_block(ids, block, step, far):
    step_x, step_y = step
    size = block[3:4] + far
    if not (step_x or step_y):
        return jnp.where(ids == 3, size, block)
    flow = block[7:8]
    if step_x:
        size = size + 2.0 * step_x * block[0:1]
        flow = flow + float(step_x) * block[4:5]
    if step_y:
        size = size + 2.0 * step_y * block[1:2]
        flow = flow + float(step_y) * block[5:6]
    size = size + float(step_x * step_x + step_y * step_y)
    moved = block + at_row(ids, r0=float(step_x), r1=float(step_y))
    return jnp.where(ids == 3, size, jnp.where(ids == 7, flow, moved))


def right_side(ids, block):
    high = rounded(block)
    rest = block - high
    low = rest - rounded(rest)
    last = jnp.where((ids == 3) | (ids == 7), low, 1.0)
    return jnp.concatenate([high, rest, last, high], axis=0).astype(jnp.bfloat16)


def left_side(ids, form, own):
    high = rounded(form)
    own_high = rounded(own)
    own_rest = own - own_high
    own_middle = rounded(own_rest)
    last = jnp.where((ids == 3) | (ids == 7), form, 0.0)
    last = last + at_row(ids, r0=own_high, r1=own_middle, r2=own_rest - own_middle)
    return [high, high, last, form - high]


def size_form(ids, block):
    return jnp.where(ids < 3, -2.0 * block, jnp.where(ids == 3, 1.0, 0.0)), block[3:4]


def flow_form(ids, block):
    swapped = pltpu.roll(block, 4, 0)
    return jnp.where(ids == 7, -1.0, jnp.where(ids == 3, 0.0, swapped)), -block[7:8]


def split(value):
    high = value.astype(jnp.bfloat16)
    return high, (value - high.astype(jnp.float32)).astype(jnp.bfloat16)


def dot(a, b):
    return jnp.dot(a, b, preferred_element_type=jnp.float32)


def halo_parts(cells_x, cells_y):
    last = cells_y
    columns, tail = pl.ds(0, cells_x), pl.ds(1, cells_x - 1)
    return (
        ((-1, 0), (0, pl.ds(1, cells_y)), (cells_x, pl.ds(1, cells_y))),
        ((0, -1), (columns, pl.ds(1, 1)), (columns, pl.ds(last + 1, 1))),
        ((0, 1), (tail, pl.ds(last, 1)), (tail, pl.ds(0, 1))),
        ((-1, -1), (0, pl.ds(1, 1)), (cells_x, pl.ds(last + 1, 1))),
        ((-1, 1), (0, pl.ds(last, 1)), (cells_x, pl.ds(0, 1))),
    )


def step_kernel(
    sizes, far_ref, count_ref, pos_ref, vel_ref, density_ref, accel_ref,
    p_ref, r_ref, left_ref, right_ref, place_ref, turned_ref, side_ref, part_ref, total_ref,
    ghost_ref, back_ref, force_ghost_ref, force_back_ref, send_sem, recv_sem,
):
    devices_x, devices_y = sizes
    cells_x, cells_y = density_ref.shape[0], density_ref.shape[1]
    span = cells_y + 2
    ids = row_ids()
    lanes = lax.broadcasted_iota(jnp.int32, (1, 128), 1)
    me_x, me_y = lax.axis_index("gx"), lax.axis_index("gy")
    parts = halo_parts(cells_x, cells_y)

    def device(step):
        return (lax.rem(me_x + step[0] + devices_x, devices_x), lax.rem(me_y + step[1] + devices_y, devices_y))

    def forward(phase, ref):
        return [
            pltpu.make_async_remote_copy(
                src_ref=ref.at[own], dst_ref=ref.at[ghost],
                send_sem=send_sem.at[phase, n], recv_sem=recv_sem.at[phase, n],
                device_id=device(step), device_id_type=MESH,
            )
            for n, (step, own, ghost) in enumerate(parts)
        ]

    def backward(phase, source, target):
        return [
            pltpu.make_async_remote_copy(
                src_ref=source.at[ghost], dst_ref=target.at[(n,) + own],
                send_sem=send_sem.at[phase, n], recv_sem=recv_sem.at[phase, n],
                device_id=device((-step[0], -step[1])), device_id_type=MESH,
            )
            for n, (step, own, ghost) in enumerate(parts)
        ]

    barrier = pltpu.get_barrier_semaphore()
    around = [(a, b) for a in (-1, 0, 1) for b in (-1, 0, 1) if a or b]
    for step in around:
        pl.semaphore_signal(barrier, inc=1, device_id=device(step), device_id_type=MESH)

    @pl.loop(0, cells_x * cells_y // 4)
    def _(quad):
        for turn in range(4):
            x, y = quad * 4 // cells_y, quad * 4 % cells_y + turn
            place = [pos_ref[d, x, pl.ds(y, 1)] - 0.5 for d in range(3)]
            speed = [vel_ref[d, x, pl.ds(y, 1)] for d in range(3)]
            size = place[0] * place[0] + place[1] * place[1] + place[2] * place[2]
            size = size + jnp.where(lanes < count_ref[x, y], 0.0, FAR)
            flow = place[0] * speed[0] + place[1] * speed[1] + place[2] * speed[2]
            p_ref[x, y + 1] = at_row(
                ids, r0=place[0], r1=place[1], r2=place[2], r3=size, r4=speed[0], r5=speed[1], r6=speed[2], r7=flow
            )

    pl.semaphore_wait(barrier, len(around))
    halo = forward(0, p_ref)
    for copy in halo:
        copy.start()

    part_ref[...] = jnp.zeros_like(part_ref)

    def base_of(x, y):
        return at_row(ids, r0=x.astype(jnp.float32), r1=y.astype(jnp.float32))

    def prepare_left(x, y):
        cell = x * cells_y + y
        block = p_ref[x, y + 1]
        blocks = left_side(ids, *size_form(ids, block)) + left_side(ids, *flow_form(ids, block))
        left_ref[cell] = jnp.concatenate(blocks, axis=0).T.astype(jnp.bfloat16)
        here = jnp.where(ids < 3, block, jnp.where(ids == 3, 1.0, 0.0))
        high = rounded(here)
        place_ref[cell] = jnp.concatenate([high, here - high], axis=0).astype(jnp.bfloat16)

    def prepare_right(x, y):
        cell = x * cells_y + y
        for kind, (step_x, step_y) in enumerate(STEPS):
            block = p_ref[x + step_x, y + 1 + step_y]
            partner = partner_block(ids, block, (step_x, step_y), far_ref[cell * 5 + kind])
            right_ref[cell * 5 + kind] = right_side(ids, partner)

    def prepare_turned(x, line):
        here = jnp.where(ids < 3, p_ref[x, line] + base_of(x, line), jnp.where(ids == 3, 1.0, 0.0))
        high = rounded(here)
        rest = here - high
        middle = rounded(rest)
        zeros = jnp.zeros((8, 128), jnp.float32)
        stacked = jnp.concatenate([high, middle, rest - middle, zeros], axis=0)
        turned_ref[x * span + line] = stacked.T.astype(jnp.bfloat16)

    def inner(count, body):
        @pl.loop(0, (cells_x - 1) * (cells_y - 2) // count)
        def _(step):
            first = step * count
            x = first // (cells_y - 2)
            body([(x, first % (cells_y - 2) + 1 + turn) for turn in range(count)])

    def outer(body):
        @pl.loop(0, cells_y // 2)
        def _(step):
            body([(cells_x - 1, step * 2), (cells_x - 1, step * 2 + 1)])

        @pl.loop(0, cells_x - 1)
        def _(x):
            body([(x, 0), (x, cells_y - 1)])

    def own_cells(count, body):
        @pl.loop(0, cells_x * cells_y // count)
        def _(step):
            first = step * count
            for turn in range(count):
                body(first // cells_y, first % cells_y + turn)

    def each(body):
        def run(chosen):
            for x, y in chosen:
                body(x, y)

        return run

    def as_int(value):
        return jnp.int32(value) if isinstance(value, int) else value

    def both(x, y):
        prepare_left(x, y)
        prepare_turned(as_int(x), y + 1)

    own_cells(4, both)
    inner(2, each(prepare_right))

    def density_cells(chosen):
        for x, y in chosen:
            cell = x * cells_y + y
            home = x * span + y + 1 + MARGIN
            left = left_ref[cell, :, :32]
            total = None
            for kinds in ((0, 1), (2, 3), (4,)):
                squares = dot(left, jnp.concatenate([right_ref[cell * 5 + kind] for kind in kinds], axis=1))
                for turn, kind in enumerate(kinds):
                    safe = jnp.maximum(squares[:, 128 * turn : 128 * turn + 128], TINY)
                    near = jnp.maximum(1.0 - safe * lax.rsqrt(safe), 0.0)
                    two = near * near
                    weight = two * two * (5.0 - 4.0 * near)
                    part_ref[kind, home] = jnp.sum(weight.reshape(16, 8, 128), axis=0)
                    if kind:
                        total = weight if total is None else total + weight
            total_ref[cell] = total

    def density_rows(x, y):
        turned = total_ref[x * cells_y + y].T
        part_ref[0, x * span + y + 1 + MARGIN] += jnp.sum(turned.reshape(16, 8, 128), axis=0)

    def gathered(x, line, count):
        sums = None
        for kind, (step_x, step_y) in enumerate(STEPS):
            first = MARGIN + (x - step_x) * span + line - step_y
            piece = part_ref[kind, pl.ds(first, count)]
            sums = piece if sums is None else sums + piece
        return sums

    def collect_ghosts(target):
        @pl.loop(0, cells_y // 8)
        def _(block):
            line = block * 8 + 1
            target[cells_x, pl.ds(line, 8)] = gathered(cells_x, line, 8)

        @pl.loop(0, cells_x + 1)
        def _(x):
            target[x, pl.ds(cells_y + 1, 1)] = gathered(x, cells_y + 1, 1)

        @pl.loop(1, cells_x + 1)
        def _(x):
            target[x, pl.ds(0, 1)] = gathered(x, 0, 1)

    def add_returned(source):
        def add(n, x, line):
            part_ref[0, x * span + line + MARGIN] += source[n, x, line]

        @pl.loop(1, cells_y + 1)
        def _(line):
            add(0, 0, line)

        @pl.loop(0, cells_x)
        def _(x):
            add(1, x, 1)

        @pl.loop(1, cells_x)
        def _(x):
            add(2, x, cells_y)

        add(3, 0, 1)
        add(4, 0, cells_y)

    def outer_turned():
        @pl.loop(0, span // 2)
        def _(pair):
            prepare_turned(jnp.int32(cells_x), pair * 2)
            prepare_turned(jnp.int32(cells_x), pair * 2 + 1)

        @pl.loop(1, cells_x)
        def _(x):
            prepare_turned(x, jnp.int32(0))
            prepare_turned(x, jnp.int32(cells_y + 1))

        prepare_turned(jnp.int32(0), jnp.int32(cells_y + 1))

    inner(2, density_cells)
    for copy in halo:
        copy.wait_recv()
    outer(each(prepare_right))
    outer(density_cells)
    collect_ghosts(ghost_ref)
    returned = backward(1, ghost_ref, back_ref)
    for copy in returned:
        copy.start()
    own_cells(4, density_rows)
    outer_turned()
    for copy in returned:
        copy.wait_recv()
    add_returned(back_ref)

    @pl.loop(0, cells_x * cells_y // 8)
    def _(block):
        x, y = block * 8 // cells_y, block * 8 % cells_y
        sums = (PARTICLE_MASS * NORMAL) * jnp.sum(gathered(x, y + 1, 8), axis=1)
        filled = p_ref[x, pl.ds(y + 1, 8)][:, 3] < 0.5 * FAR
        density = jnp.where(filled, sums, 0.0)
        first = pl.multiple_of(y, 8)
        density_ref[x, pl.ds(first, 8)] = density
        safe_rho = jnp.where(filled, density, 1.0)
        term = SOUND_SPEED * SOUND_SPEED * (safe_rho - REST_DENSITY) / (safe_rho * safe_rho)
        scaled = safe_rho * (1.0 / (VISCOUS * SOUND_SPEED * 2.0 * SMOOTH))
        for turn in range(8):
            pair = at_row(ids, r0=scaled[turn : turn + 1], r1=term[turn : turn + 1])
            r_ref[x, y + 1 + turn] = pair
            side_ref[x * cells_y + y + turn] = pair.T

    densities = forward(2, r_ref)
    for copy in densities:
        copy.start()

    def force_cells(chosen):
        empty = jnp.zeros((32, 128), jnp.bfloat16)
        for x, y in chosen:
            cell = x * cells_y + y
            home = x * span + y + 1
            left = left_ref[cell]
            own = place_ref[cell]
            rho_i = jnp.broadcast_to(side_ref[cell, :, 0:1], (128, 128))
            term_i = jnp.broadcast_to(side_ref[cell, :, 1:2], (128, 128))
            highs, lows, places = [], [], []
            for kind, (step_x, step_y) in enumerate(STEPS):
                side = right_ref[cell * 5 + kind]
                upper = jnp.concatenate([side, empty], axis=1)
                lower = jnp.concatenate([empty, side], axis=1)
                forms = dot(left, jnp.concatenate([upper, lower], axis=0))
                other = r_ref[x + step_x, y + 1 + step_y]
                safe = jnp.maximum(forms[:, :128], TINY)
                near = jnp.maximum(1.0 - safe * lax.rsqrt(safe), 0.0)
                cubed = near * near * near
                bottom = (safe + 0.01 * SMOOTH * SMOOTH) * (rho_i + other[0:1])
                damping = jnp.maximum(forms[:, 128:], 0.0) * pl.reciprocal(bottom, approx=True)
                scalar = (term_i + other[1:2] + damping) * cubed
                high, low = split(scalar)
                column = dot(own, high) + dot(own, low)
                column = column[:8] + column[8:]
                if kind:
                    column = column - at_row(ids, r0=float(step_x), r1=float(step_y)) * column[3:4]
                    highs.append(high)
                    lows.append(low)
                    places.append(turned_ref[home + step_x * span + step_y])
                part_ref[kind, home + MARGIN] = column
            streams = jnp.concatenate([jnp.concatenate(highs, axis=1), jnp.concatenate(lows, axis=1)], axis=0)
            sums = dot(streams, jnp.concatenate(places, axis=0))
            total_ref[cell, :, :32] = sums[:128] + sums[128:]

    def force_rows(x, y):
        sums = total_ref[x * cells_y + y, :, :32].T
        sums = sums[0:8] + sums[8:16] + sums[16:24]
        part_ref[0, x * span + y + 1 + MARGIN] += sums - base_of(x, y + 1) * sums[3:4]

    inner(2, force_cells)
    for copy in densities:
        copy.wait_recv()
    outer(force_cells)
    collect_ghosts(force_ghost_ref)
    forces_back = backward(3, force_ghost_ref, force_back_ref)
    for copy in forces_back:
        copy.start()
    own_cells(4, force_rows)
    for copy in forces_back:
        copy.wait_recv()
    add_returned(force_back_ref)
    scale = PARTICLE_MASS * 5.0 * NORMAL / (SMOOTH * SMOOTH)

    @pl.loop(0, cells_x * cells_y // 8)
    def _(block):
        x, y = block * 8 // cells_y, block * 8 % cells_y
        sums = gathered(x, y + 1, 8)
        here = p_ref[x, pl.ds(y + 1, 8)]
        filled = here[:, 3] < 0.5 * FAR
        force = scale * (here * sums[:, 3:4] - sums)
        first = pl.multiple_of(y, 8)
        for d in range(3):
            accel = force[:, d] - GRAVITY if d == 2 else force[:, d]
            accel_ref[d, x, pl.ds(first, 8)] = jnp.where(filled, accel, 0.0)

    for copy in halo + returned + densities + forces_back:
        copy.wait_send()


def call_step(sizes, far, counts, positions, velocities):
    _, cells_x, cells_y, slots = positions.shape
    own, span = cells_x * cells_y, cells_y + 2
    total = (cells_x + 1) * span
    grid = (cells_x + 1, span, 8, slots)
    f32, bf16 = jnp.float32, jnp.bfloat16
    return pl.pallas_call(
        functools.partial(step_kernel, sizes),
        out_shape=(
            jax.ShapeDtypeStruct((cells_x, cells_y, slots), f32),
            jax.ShapeDtypeStruct((3, cells_x, cells_y, slots), f32),
        ),
        in_specs=[pl.BlockSpec(memory_space=pltpu.SMEM)] * 2 + [pl.BlockSpec(memory_space=pltpu.VMEM)] * 2,
        out_specs=(pl.BlockSpec(memory_space=pltpu.VMEM), pl.BlockSpec(memory_space=pltpu.VMEM)),
        scratch_shapes=[
            pltpu.VMEM(grid, f32),
            pltpu.VMEM(grid, f32),
            pltpu.VMEM((own, 128, 64), bf16),
            pltpu.VMEM((own * 5, 32, 128), bf16),
            pltpu.VMEM((own, 16, 128), bf16),
            pltpu.VMEM((total, 128, 32), bf16),
            pltpu.VMEM((own, 128, 8), f32),
            pltpu.VMEM((5, total + MARGIN + 8, 8, 128), f32),
            pltpu.VMEM((own, 128, 128), f32),
            pltpu.VMEM(grid, f32),
            pltpu.VMEM((5,) + grid, f32),
            pltpu.VMEM(grid, f32),
            pltpu.VMEM((5,) + grid, f32),
            pltpu.SemaphoreType.DMA((4, 5)),
            pltpu.SemaphoreType.DMA((4, 5)),
        ],
        compiler_params=pltpu.CompilerParams(
            vmem_limit_bytes=VMEM_BYTES, collective_id=0, has_side_effects=True
        ),
        name="step",
    )(far, counts, positions, velocities)


def per_device(sizes, positions, velocities, counts, cell_pairs, pair_count):
    codes = cell_pairs.reshape(-1)
    width = codes.shape[0]
    listed = jnp.arange(width, dtype=jnp.int32) < pair_count.reshape(())
    every = jnp.arange(positions.shape[1] * positions.shape[2] * 5, dtype=jnp.int32)
    named = jnp.any((codes[:, None] == every[None, :]) & listed[:, None], axis=0)
    far = jnp.where(named, 0.0, FAR).astype(jnp.float32)
    return call_step(sizes, far, counts, positions, velocities)


def solution(mesh):
    placed = (
        P(None, "gx", "gy", None),
        P(None, "gx", "gy", None),
        P("gx", "gy"),
        P("gx", "gy", None),
        P("gx", "gy"),
    )
    sizes = (mesh.shape["gx"], mesh.shape["gy"])
    return jax.shard_map(
        functools.partial(per_device, sizes),
        mesh=mesh,
        in_specs=placed,
        out_specs=(P("gx", "gy", None), P(None, "gx", "gy", None)),
        check_vma=False,
    )
```

time: 251 us -> 140 us (0.56)
  the two profiles are of different devices: /device:TPU:30 before, /device:TPU:24 now
where the time goes in v3:
time: 140 us
  Pallas kernels  134 us (96%)
  local copies, waits for them, and re-layouts  3.09 us (2%)
  other arithmetic  1.6 us (1%)
    pallas_call x1, Pallas kernels, call_step(): pl.pallas_call(functools.partial(step_kernel, sizes), out_shape=(jax.Shap...  134 us
    unnamed x2, local copies, waits for them, and re-layouts  3.09 us

profile of v3, /device:TPU:24, one launch (start us, length us, event | category | flops | bytes accessed | tf_op | source)
XLA Modules:
  0.0 139.8 jit_solution(18254103427829497847)
XLA Ops:
  1.3 0.7 reduce
  2.0 0.3 fusion.1
  2.3 0.6 broadcast_select_fusion.far_ref
  2.9 133.8 %step.1 = (f32[4,32,128]{2,1,0:T(8,128)}, f32[3,4,32,128]{3,2,1,0:T(8,128)}) custom-call(f32[640]{0:T(1024)} %broadcast_select_fusion.far_ref, s32[4,32]{1,0:T(4,128)} %count_ref.1, f32[3,4,32,128]{3,2,1,0:T(8,128)} %pos_ref.1, f32[3,4,32,128]{3,2,1,0:T(8,128)} %vel_ref.1), custom_call_target="tpu_custom_call" | custom-call | tf_op jit(solution)/shard_map/step/pallas_call | solution.py:421
  136.7 1.5 %copy.10 = f32[4,32,128]{2,1,0:T(8,128)} copy(f32[4,32,128]{2,1,0:T(8,128)} %get-tuple-element.4) | data formatting | bytes 131072
  138.1 1.6 %copy.11 = f32[3,4,32,128]{3,2,1,0:T(8,128)} copy(f32[3,4,32,128]{3,2,1,0:T(8,128)} %get-tuple-element.5) | data formatting | bytes 393216
  (1 shorter events, 0.0 us)

commit v4 on v3

--- a/solution.py
+++ b/solution.py
@@ -18,6 +18,8 @@
 FAR = 1.0e4
 TINY = 1.0e-12
 MARGIN = 40
+TOGETHER = 6
+LATER = 2
 VMEM_BYTES = 56 * 1024 * 1024
 MESH = pl.DeviceIdType.MESH
 
@@ -39,19 +41,16 @@
 
 def partner_block(ids, block, step, far):
     step_x, step_y = step
-    size = block[3:4] + far
+    shift = at_row(ids, r0=float(step_x), r1=float(step_y), r3=far + float(step_x * step_x + step_y * step_y))
     if not (step_x or step_y):
-        return jnp.where(ids == 3, size, block)
-    flow = block[7:8]
+        return block + shift
+    turn = None
     if step_x:
-        size = size + 2.0 * step_x * block[0:1]
-        flow = flow + float(step_x) * block[4:5]
+        turn = pltpu.roll(block, 3, 0)
     if step_y:
-        size = size + 2.0 * step_y * block[1:2]
-        flow = flow + float(step_y) * block[5:6]
-    size = size + float(step_x * step_x + step_y * step_y)
-    moved = block + at_row(ids, r0=float(step_x), r1=float(step_y))
-    return jnp.where(ids == 3, size, jnp.where(ids == 7, flow, moved))
+        line = pltpu.roll(block, 2, 0)
+        turn = line if turn is None else turn + line if step_y > 0 else turn - line
+    return block + shift + turn * at_row(ids, r3=2.0, r7=1.0)
 
 
 def right_side(ids, block):
@@ -104,7 +103,7 @@
 
 def step_kernel(
     sizes, far_ref, count_ref, pos_ref, vel_ref, density_ref, accel_ref,
-    p_ref, r_ref, left_ref, right_ref, place_ref, turned_ref, side_ref, part_ref, total_ref,
+    p_ref, r_ref, left_ref, right_ref, place_ref, turned_ref, side_ref, part_ref, total_ref, sums_ref,
     ghost_ref, back_ref, force_ghost_ref, force_back_ref, send_sem, recv_sem,
 ):
     devices_x, devices_y = sizes
@@ -156,11 +155,6 @@
                 ids, r0=place[0], r1=place[1], r2=place[2], r3=size, r4=speed[0], r5=speed[1], r6=speed[2], r7=flow
             )
 
-    pl.semaphore_wait(barrier, len(around))
-    halo = forward(0, p_ref)
-    for copy in halo:
-        copy.start()
-
     part_ref[...] = jnp.zeros_like(part_ref)
 
     def base_of(x, y):
@@ -191,21 +185,21 @@
         stacked = jnp.concatenate([high, middle, rest - middle, zeros], axis=0)
         turned_ref[x * span + line] = stacked.T.astype(jnp.bfloat16)
 
-    def inner(count, body):
-        @pl.loop(0, (cells_x - 1) * (cells_y - 2) // count)
+    def inner(columns, count, body):
+        first_x, last_x = columns
+
+        @pl.loop(0, (last_x - first_x) * (cells_y - 2) // count)
         def _(step):
             first = step * count
-            x = first // (cells_y - 2)
+            x = first_x + first // (cells_y - 2)
             body([(x, first % (cells_y - 2) + 1 + turn) for turn in range(count)])
 
-    def outer(body):
-        @pl.loop(0, cells_y // 2)
+    def outer(count, body):
+        @pl.loop(0, cells_y // count)
         def _(step):
-            body([(cells_x - 1, step * 2), (cells_x - 1, step * 2 + 1)])
-
-        @pl.loop(0, cells_x - 1)
-        def _(x):
-            body([(x, 0), (x, cells_y - 1)])
+            body([(cells_x - 1, step * count + turn) for turn in range(count)])
+
+        body([(x, y) for x in range(cells_x - 1) for y in (0, cells_y - 1)])
 
     def own_cells(count, body):
         @pl.loop(0, cells_x * cells_y // count)
@@ -227,9 +221,6 @@
     def both(x, y):
         prepare_left(x, y)
         prepare_turned(as_int(x), y + 1)
-
-    own_cells(4, both)
-    inner(2, each(prepare_right))
 
     def density_cells(chosen):
         for x, y in chosen:
@@ -243,15 +234,23 @@
                     safe = jnp.maximum(squares[:, 128 * turn : 128 * turn + 128], TINY)
                     near = jnp.maximum(1.0 - safe * lax.rsqrt(safe), 0.0)
                     two = near * near
-                    weight = two * two * (5.0 - 4.0 * near)
+                    weight = two * two * (1.25 - near)
                     part_ref[kind, home] = jnp.sum(weight.reshape(16, 8, 128), axis=0)
                     if kind:
                         total = weight if total is None else total + weight
             total_ref[cell] = total
 
-    def density_rows(x, y):
-        turned = total_ref[x * cells_y + y].T
-        part_ref[0, x * span + y + 1 + MARGIN] += jnp.sum(turned.reshape(16, 8, 128), axis=0)
+    def density_rows():
+        def collect(step, columns):
+            for turn in range(4):
+                cell = step * 4 + turn
+                sums = jnp.sum(total_ref[cell], axis=1, keepdims=True)
+                columns = jnp.where(lanes == cell, sums, columns)
+            return columns
+
+        cells = cells_x * cells_y
+        columns = lax.fori_loop(0, cells // 4, collect, jnp.zeros((128, cells), jnp.float32))
+        sums_ref[...] = columns.T
 
     def gathered(x, line, count):
         sums = None
@@ -307,16 +306,23 @@
 
         prepare_turned(jnp.int32(0), jnp.int32(cells_y + 1))
 
-    inner(2, density_cells)
+    own_cells(4, both)
+    inner((0, cells_x - 1), 5, each(prepare_right))
+    pl.semaphore_wait(barrier, len(around))
+    halo = forward(0, p_ref)
+    for copy in halo:
+        copy.start()
+    inner((0, cells_x - 2), TOGETHER, density_cells)
     for copy in halo:
         copy.wait_recv()
-    outer(each(prepare_right))
-    outer(density_cells)
+    outer(4, each(prepare_right))
+    outer(8, density_cells)
     collect_ghosts(ghost_ref)
     returned = backward(1, ghost_ref, back_ref)
     for copy in returned:
         copy.start()
-    own_cells(4, density_rows)
+    inner((cells_x - 2, cells_x - 1), TOGETHER, density_cells)
+    density_rows()
     outer_turned()
     for copy in returned:
         copy.wait_recv()
@@ -325,7 +331,8 @@
     @pl.loop(0, cells_x * cells_y // 8)
     def _(block):
         x, y = block * 8 // cells_y, block * 8 % cells_y
-        sums = (PARTICLE_MASS * NORMAL) * jnp.sum(gathered(x, y + 1, 8), axis=1)
+        sums = jnp.sum(gathered(x, y + 1, 8), axis=1) + sums_ref[pl.ds(pl.multiple_of(block * 8, 8), 8)]
+        sums = (4.0 * PARTICLE_MASS * NORMAL) * sums
         filled = p_ref[x, pl.ds(y + 1, 8)][:, 3] < 0.5 * FAR
         density = jnp.where(filled, sums, 0.0)
         first = pl.multiple_of(y, 8)
@@ -344,52 +351,80 @@
 
     def force_cells(chosen):
         empty = jnp.zeros((32, 128), jnp.bfloat16)
-        for x, y in chosen:
+        units = [(place, kind) for place in range(len(chosen)) for kind in range(5)]
+
+        def forms_of(unit):
+            place, kind = unit
+            x, y = chosen[place]
             cell = x * cells_y + y
-            home = x * span + y + 1
-            left = left_ref[cell]
-            own = place_ref[cell]
+            side = right_ref[cell * 5 + kind]
+            upper = jnp.concatenate([side, empty], axis=1)
+            lower = jnp.concatenate([empty, side], axis=1)
+            return dot(left_ref[cell], jnp.concatenate([upper, lower], axis=0))
+
+        def scalar_of(unit, forms):
+            place, kind = unit
+            x, y = chosen[place]
+            cell = x * cells_y + y
+            step_x, step_y = STEPS[kind]
+            other = r_ref[x + step_x, y + 1 + step_y]
             rho_i = jnp.broadcast_to(side_ref[cell, :, 0:1], (128, 128))
             term_i = jnp.broadcast_to(side_ref[cell, :, 1:2], (128, 128))
-            highs, lows, places = [], [], []
-            for kind, (step_x, step_y) in enumerate(STEPS):
-                side = right_ref[cell * 5 + kind]
-                upper = jnp.concatenate([side, empty], axis=1)
-                lower = jnp.concatenate([empty, side], axis=1)
-                forms = dot(left, jnp.concatenate([upper, lower], axis=0))
-                other = r_ref[x + step_x, y + 1 + step_y]
-                safe = jnp.maximum(forms[:, :128], TINY)
-                near = jnp.maximum(1.0 - safe * lax.rsqrt(safe), 0.0)
-                cubed = near * near * near
-                bottom = (safe + 0.01 * SMOOTH * SMOOTH) * (rho_i + other[0:1])
-                damping = jnp.maximum(forms[:, 128:], 0.0) * pl.reciprocal(bottom, approx=True)
-                scalar = (term_i + other[1:2] + damping) * cubed
-                high, low = split(scalar)
-                column = dot(own, high) + dot(own, low)
-                column = column[:8] + column[8:]
-                if kind:
-                    column = column - at_row(ids, r0=float(step_x), r1=float(step_y)) * column[3:4]
-                    highs.append(high)
-                    lows.append(low)
-                    places.append(turned_ref[home + step_x * span + step_y])
-                part_ref[kind, home + MARGIN] = column
+            safe = jnp.maximum(forms[:, :128], TINY)
+            near = jnp.maximum(1.0 - safe * lax.rsqrt(safe), 0.0)
+            cubed = near * near * near
+            bottom = (safe + 0.01 * SMOOTH * SMOOTH) * (rho_i + other[0:1])
+            damping = jnp.maximum(forms[:, 128:], 0.0) * pl.reciprocal(bottom, approx=True)
+            return split((term_i + other[1:2] + damping) * cubed)
+
+        def columns(unit, high, low):
+            place, kind = unit
+            x, y = chosen[place]
+            step_x, step_y = STEPS[kind]
+            own = place_ref[x * cells_y + y]
+            column = dot(own, high) + dot(own, low)
+            column = column[:8] + column[8:]
+            if kind:
+                column = column - at_row(ids, r0=float(step_x), r1=float(step_y)) * column[3:4]
+            part_ref[kind, x * span + y + 1 + MARGIN] = column
+
+        def rows(place, highs, lows):
+            x, y = chosen[place]
+            home = x * span + y + 1
             streams = jnp.concatenate([jnp.concatenate(highs, axis=1), jnp.concatenate(lows, axis=1)], axis=0)
+            places = [turned_ref[home + STEPS[k][0] * span + STEPS[k][1]] for k in range(1, 5)]
             sums = dot(streams, jnp.concatenate(places, axis=0))
-            total_ref[cell, :, :32] = sums[:128] + sums[128:]
+            total_ref[x * cells_y + y, :, :32] = sums[:128] + sums[128:]
+
+        highs, lows, pending = [], [], []
+        for turn, unit in enumerate(units):
+            high, low = scalar_of(unit, forms_of(unit))
+            columns(unit, high, low)
+            if unit[1]:
+                highs.append(high)
+                lows.append(low)
+            if unit[1] == 4:
+                pending.append((turn + LATER, unit[0], highs, lows))
+                highs, lows = [], []
+            while pending and pending[0][0] <= turn:
+                rows(*pending.pop(0)[1:])
+        for _, *job in pending:
+            rows(*job)
 
     def force_rows(x, y):
         sums = total_ref[x * cells_y + y, :, :32].T
         sums = sums[0:8] + sums[8:16] + sums[16:24]
         part_ref[0, x * span + y + 1 + MARGIN] += sums - base_of(x, y + 1) * sums[3:4]
 
-    inner(2, force_cells)
+    inner((0, cells_x - 2), TOGETHER, force_cells)
     for copy in densities:
         copy.wait_recv()
-    outer(force_cells)
+    outer(8, force_cells)
     collect_ghosts(force_ghost_ref)
     forces_back = backward(3, force_ghost_ref, force_back_ref)
     for copy in forces_back:
         copy.start()
+    inner((cells_x - 2, cells_x - 1), TOGETHER, force_cells)
     own_cells(4, force_rows)
     for copy in forces_back:
         copy.wait_recv()
@@ -436,6 +471,7 @@
             pltpu.VMEM((own, 128, 8), f32),
             pltpu.VMEM((5, total + MARGIN + 8, 8, 128), f32),
             pltpu.VMEM((own, 128, 128), f32),
+            pltpu.VMEM((own, 128), f32),
             pltpu.VMEM(grid, f32),
             pltpu.VMEM((5,) + grid, f32),
             pltpu.VMEM(grid, f32),

time: 140 us -> 104 us (0.74); the launches traced: 140 us -> 102 us
  Pallas kernels: 134 us -> 96.3 us
    pallas_call x1, Pallas kernels: 134 us -> 96.3 us  [call_step(): pl.pallas_call(functools.partial(step_kernel, sizes), out_shape=(jax.Shap...]
where the time goes in v4:
time: 104 us; the launch traced here: 102 us
  Pallas kernels  96.3 us (93%)
  local copies, waits for them, and re-layouts  3.09 us (3%)
  other arithmetic  1.6 us (2%)
  between operations  1.3 us (1%)
    pallas_call x1, Pallas kernels, call_step(): pl.pallas_call(functools.partial(step_kernel, sizes), out_shape=(jax.Shap...  96.3 us
    unnamed x2, local copies, waits for them, and re-layouts  3.09 us

profile of v4, /device:TPU:24, one launch (start us, length us, event | category | flops | bytes accessed | tf_op | source)
XLA Modules:
  0.0 102.3 jit_solution(5965641176301857907)
XLA Ops:
  1.3 0.7 reduce
  2.0 0.3 fusion.1
  2.3 0.6 broadcast_select_fusion.far_ref
  2.9 96.3 %step.1 = (f32[4,32,128]{2,1,0:T(8,128)}, f32[3,4,32,128]{3,2,1,0:T(8,128)}) custom-call(f32[640]{0:T(1024)} %broadcast_select_fusion.far_ref, s32[4,32]{1,0:T(4,128)} %count_ref.1, f32[3,4,32,128]{3,2,1,0:T(8,128)} %pos_ref.1, f32[3,4,32,128]{3,2,1,0:T(8,128)} %vel_ref.1), custom_call_target="tpu_custom_call" | custom-call | tf_op jit(solution)/shard_map/step/pallas_call | solution.py:456
  99.2 1.5 %copy.10 = f32[4,32,128]{2,1,0:T(8,128)} copy(f32[4,32,128]{2,1,0:T(8,128)} %get-tuple-element.4) | data formatting | bytes 131072
  100.7 1.6 %copy.11 = f32[3,4,32,128]{3,2,1,0:T(8,128)} copy(f32[3,4,32,128]{3,2,1,0:T(8,128)} %get-tuple-element.5) | data formatting | bytes 393216
  (1 shorter events, 0.0 us)

commit v5 on v4

--- a/solution.py
+++ b/solution.py
@@ -18,7 +18,7 @@
 FAR = 1.0e4
 TINY = 1.0e-12
 MARGIN = 40
-TOGETHER = 6
+TOGETHER = 10
 LATER = 2
 VMEM_BYTES = 56 * 1024 * 1024
 MESH = pl.DeviceIdType.MESH
@@ -103,7 +103,7 @@
 
 def step_kernel(
     sizes, far_ref, count_ref, pos_ref, vel_ref, density_ref, accel_ref,
-    p_ref, r_ref, left_ref, right_ref, place_ref, turned_ref, side_ref, part_ref, total_ref, sums_ref,
+    p_ref, r_ref, left_ref, right_ref, place_ref, turned_ref, part_ref, total_ref, sums_ref,
     ghost_ref, back_ref, force_ghost_ref, force_back_ref, send_sem, recv_sem,
 ):
     devices_x, devices_y = sizes
@@ -242,14 +242,14 @@
 
     def density_rows():
         def collect(step, columns):
-            for turn in range(4):
-                cell = step * 4 + turn
+            for turn in range(8):
+                cell = step * 8 + turn
                 sums = jnp.sum(total_ref[cell], axis=1, keepdims=True)
                 columns = jnp.where(lanes == cell, sums, columns)
             return columns
 
         cells = cells_x * cells_y
-        columns = lax.fori_loop(0, cells // 4, collect, jnp.zeros((128, cells), jnp.float32))
+        columns = lax.fori_loop(0, cells // 8, collect, jnp.zeros((128, cells), jnp.float32))
         sums_ref[...] = columns.T
 
     def gathered(x, line, count):
@@ -306,7 +306,7 @@
 
         prepare_turned(jnp.int32(0), jnp.int32(cells_y + 1))
 
-    own_cells(4, both)
+    own_cells(8, both)
     inner((0, cells_x - 1), 5, each(prepare_right))
     pl.semaphore_wait(barrier, len(around))
     halo = forward(0, p_ref)
@@ -341,9 +341,7 @@
         term = SOUND_SPEED * SOUND_SPEED * (safe_rho - REST_DENSITY) / (safe_rho * safe_rho)
         scaled = safe_rho * (1.0 / (VISCOUS * SOUND_SPEED * 2.0 * SMOOTH))
         for turn in range(8):
-            pair = at_row(ids, r0=scaled[turn : turn + 1], r1=term[turn : turn + 1])
-            r_ref[x, y + 1 + turn] = pair
-            side_ref[x * cells_y + y + turn] = pair.T
+            r_ref[x, y + 1 + turn] = at_row(ids, r0=scaled[turn : turn + 1], r1=term[turn : turn + 1])
 
     densities = forward(2, r_ref)
     for copy in densities:
@@ -368,8 +366,7 @@
             cell = x * cells_y + y
             step_x, step_y = STEPS[kind]
             other = r_ref[x + step_x, y + 1 + step_y]
-            rho_i = jnp.broadcast_to(side_ref[cell, :, 0:1], (128, 128))
-            term_i = jnp.broadcast_to(side_ref[cell, :, 1:2], (128, 128))
+            rho_i, term_i = sides[place]
             safe = jnp.maximum(forms[:, :128], TINY)
             near = jnp.maximum(1.0 - safe * lax.rsqrt(safe), 0.0)
             cubed = near * near * near
@@ -396,6 +393,10 @@
             sums = dot(streams, jnp.concatenate(places, axis=0))
             total_ref[x * cells_y + y, :, :32] = sums[:128] + sums[128:]
 
+        sides = []
+        for x, y in chosen:
+            turned = r_ref[x, y + 1].T
+            sides.append([jnp.broadcast_to(turned[:, d : d + 1], (128, 128)) for d in range(2)])
         highs, lows, pending = [], [], []
         for turn, unit in enumerate(units):
             high, low = scalar_of(unit, forms_of(unit))
@@ -425,7 +426,7 @@
     for copy in forces_back:
         copy.start()
     inner((cells_x - 2, cells_x - 1), TOGETHER, force_cells)
-    own_cells(4, force_rows)
+    own_cells(8, force_rows)
     for copy in forces_back:
         copy.wait_recv()
     add_returned(force_back_ref)
@@ -468,7 +469,6 @@
             pltpu.VMEM((own * 5, 32, 128), bf16),
             pltpu.VMEM((own, 16, 128), bf16),
             pltpu.VMEM((total, 128, 32), bf16),
-            pltpu.VMEM((own, 128, 8), f32),
             pltpu.VMEM((5, total + MARGIN + 8, 8, 128), f32),
             pltpu.VMEM((own, 128, 128), f32),
             pltpu.VMEM((own, 128), f32),
@@ -486,6 +486,27 @@
     )(far, counts, positions, velocities)
 
 
+def finish_kernel(density_ref, accel_ref, density_out, accel_out, sems):
+    first = pltpu.make_async_copy(density_ref, density_out, sems.at[0])
+    second = pltpu.make_async_copy(accel_ref, accel_out, sems.at[1])
+    second.start()
+    first.start()
+    second.wait()
+    first.wait()
+
+
+def call_finish(density, accel):
+    return pl.pallas_call(
+        finish_kernel,
+        out_shape=tuple(jax.ShapeDtypeStruct(a.shape, a.dtype) for a in (density, accel)),
+        in_specs=[pl.BlockSpec(memory_space=pl.ANY)] * 2,
+        out_specs=(pl.BlockSpec(memory_space=pl.ANY), pl.BlockSpec(memory_space=pl.ANY)),
+        scratch_shapes=[pltpu.SemaphoreType.DMA((2,))],
+        compiler_params=pltpu.CompilerParams(vmem_limit_bytes=VMEM_BYTES),
+        name="finish",
+    )(density, accel)
+
+
 def per_device(sizes, positions, velocities, counts, cell_pairs, pair_count):
     codes = cell_pairs.reshape(-1)
     width = codes.shape[0]
@@ -493,7 +514,7 @@
     every = jnp.arange(positions.shape[1] * positions.shape[2] * 5, dtype=jnp.int32)
     named = jnp.any((codes[:, None] == every[None, :]) & listed[:, None], axis=0)
     far = jnp.where(named, 0.0, FAR).astype(jnp.float32)
-    return call_step(sizes, far, counts, positions, velocities)
+    return call_finish(*call_step(sizes, far, counts, positions, velocities))
 
 
 def solution(mesh):

time: 104 us -> 106 us (1.019)
  Pallas kernels: 96.3 us -> 101 us
  local copies, waits for them, and re-layouts: 3.09 us -> 0 us
    pallas_call x0 -> x1, Pallas kernels: none -> 9.06 us  [call_finish(): pl.pallas_call(finish_kernel, out_shape=tuple((jax.ShapeDtypeStruct(a.sha...]
    pallas_call x1, Pallas kernels: 96.3 us -> 91.7 us  [call_step(): pl.pallas_call(functools.partial(step_kernel, sizes), out_shape=(jax.Shap...]
    unnamed x2 -> x0, local copies, waits for them, and re-layouts: 3.09 us -> none
where the time goes in v5:
time: 106 us; the launch traced here: 104 us
  Pallas kernels  101 us (95%)
  other arithmetic  1.6 us (2%)
  between operations  1.46 us (1%)
    pallas_call x1, Pallas kernels, call_step(): pl.pallas_call(functools.partial(step_kernel, sizes), out_shape=(jax.Shap...  91.7 us
    pallas_call x1, Pallas kernels, call_finish(): pl.pallas_call(finish_kernel, out_shape=tuple((jax.ShapeDtypeStruct(a.sha...  9.06 us

profile of v5, /device:TPU:24, one launch (start us, length us, event | category | flops | bytes accessed | tf_op | source)
XLA Modules:
  0.0 103.8 jit_solution(8859488295596712122)
XLA Ops:
  1.3 0.7 reduce
  2.0 0.3 fusion.1
  2.3 0.6 broadcast_select_fusion.far_ref
  2.9 91.7 %step.1 = (f32[4,32,128]{2,1,0:T(8,128)}, f32[3,4,32,128]{3,2,1,0:T(8,128)}) custom-call(f32[640]{0:T(1024)} %broadcast_select_fusion.far_ref, s32[4,32]{1,0:T(4,128)} %count_ref.1, f32[3,4,32,128]{3,2,1,0:T(8,128)} %pos_ref.1, f32[3,4,32,128]{3,2,1,0:T(8,128)} %vel_ref.1), custom_call_target="tpu_custom_call" | custom-call | tf_op jit(solution)/shard_map/step/pallas_call | solution.py:457
  94.6 9.1 %finish.1 = (f32[4,32,128]{2,1,0:T(8,128)}, f32[3,4,32,128]{3,2,1,0:T(8,128)}) custom-call(f32[4,32,128]{2,1,0:T(8,128)} %get-tuple-element.4.density_ref, f32[3,4,32,128]{3,2,1,0:T(8,128)} %get-tuple-element.5.accel_ref), custom_call_target="tpu_custom_call" | custom-call | tf_op jit(solution)/shard_map/finish/pallas_call | solution.py:499
  (1 shorter events, 0.0 us)

commit v6 on v5

--- a/solution.py
+++ b/solution.py
@@ -307,7 +307,7 @@
         prepare_turned(jnp.int32(0), jnp.int32(cells_y + 1))
 
     own_cells(8, both)
-    inner((0, cells_x - 1), 5, each(prepare_right))
+    inner((0, cells_x - 1), 10, each(prepare_right))
     pl.semaphore_wait(barrier, len(around))
     halo = forward(0, p_ref)
     for copy in halo:
@@ -486,22 +486,17 @@
     )(far, counts, positions, velocities)
 
 
-def finish_kernel(density_ref, accel_ref, density_out, accel_out, sems):
-    first = pltpu.make_async_copy(density_ref, density_out, sems.at[0])
-    second = pltpu.make_async_copy(accel_ref, accel_out, sems.at[1])
-    second.start()
-    first.start()
-    second.wait()
-    first.wait()
+def finish_kernel(density_ref, accel_ref, density_out, accel_out):
+    density_out[...] = density_ref[...]
+    accel_out[...] = accel_ref[...]
 
 
 def call_finish(density, accel):
     return pl.pallas_call(
         finish_kernel,
         out_shape=tuple(jax.ShapeDtypeStruct(a.shape, a.dtype) for a in (density, accel)),
-        in_specs=[pl.BlockSpec(memory_space=pl.ANY)] * 2,
-        out_specs=(pl.BlockSpec(memory_space=pl.ANY), pl.BlockSpec(memory_space=pl.ANY)),
-        scratch_shapes=[pltpu.SemaphoreType.DMA((2,))],
+        in_specs=[pl.BlockSpec(memory_space=pltpu.VMEM)] * 2,
+        out_specs=(pl.BlockSpec(memory_space=pltpu.VMEM), pl.BlockSpec(memory_space=pltpu.VMEM)),
         compiler_params=pltpu.CompilerParams(vmem_limit_bytes=VMEM_BYTES),
         name="finish",
     )(density, accel)

time: 106 us -> 97.9 us (0.924)
  Pallas kernels: 101 us -> 93.2 us
    pallas_call x1, Pallas kernels: 9.06 us -> 1.67 us  [call_finish(): pl.pallas_call(finish_kernel, out_shape=tuple((jax.ShapeDtypeStruct(a.sha...]
where the time goes in v6:
time: 97.9 us; the launch traced here: 96.1 us
  Pallas kernels  93.2 us (95%)
  other arithmetic  1.6 us (2%)
  between operations  1.3 us (1%)
    pallas_call x1, Pallas kernels, call_step(): pl.pallas_call(functools.partial(step_kernel, sizes), out_shape=(jax.Shap...  91.5 us

profile of v6, /device:TPU:24, one launch (start us, length us, event | category | flops | bytes accessed | tf_op | source)
XLA Modules:
  0.0 96.1 jit_solution(10607539723785638527)
XLA Ops:
  1.3 0.7 reduce
  2.0 0.3 fusion.1
  2.3 0.6 broadcast_select_fusion.far_ref
  2.9 91.5 %step.1 = (f32[4,32,128]{2,1,0:T(8,128)}, f32[3,4,32,128]{3,2,1,0:T(8,128)}) custom-call(f32[640]{0:T(1024)} %broadcast_select_fusion.far_ref, s32[4,32]{1,0:T(4,128)} %count_ref.1, f32[3,4,32,128]{3,2,1,0:T(8,128)} %pos_ref.1, f32[3,4,32,128]{3,2,1,0:T(8,128)} %vel_ref.1), custom_call_target="tpu_custom_call" | custom-call | tf_op jit(solution)/shard_map/step/pallas_call | solution.py:457
  94.4 1.7 %finish.1 = (f32[4,32,128]{2,1,0:T(8,128)}, f32[3,4,32,128]{3,2,1,0:T(8,128)}) custom-call(f32[4,32,128]{2,1,0:T(8,128)} %get-tuple-element.4.density_ref, f32[3,4,32,128]{3,2,1,0:T(8,128)} %get-tuple-element.5.accel_ref), custom_call_target="tpu_custom_call" | custom-call | tf_op jit(solution)/shard_map/finish/pallas_call | solution.py:495
  (1 shorter events, 0.0 us)
